TPU v7x, 32 devices: a whole 2x2x4 slice. The times are simulated.
32 devices in a mesh: section: 2 (over x), dp: 4 (over z), tensor: 4 (over y, core).
Axes of the slice: x: 2, y: 2, z: 4, core: 2. Of those that a mesh axis runs over, the one named last changes fastest.
Arguments:
- decoder_in: bfloat16 [16384, 1024], P(('section', 'dp'), 'tensor'), may hold values from -6 to 6
- encoder_out: bfloat16 [16384, 1024], P(('section', 'dp'), 'tensor'), may hold values from -6 to 6
- segments: int32 [8, 2048], P(('section', 'dp')), may hold values from 0 to 5, never falling along the last dimension, each value on 1 to 1024 neighbouring positions
- w_skip: bfloat16 [2, 1024, 1024], P(None, 'tensor'), may hold values from -0.125 to 0.125
- b_skip: float32 [1024], replicated, may hold values from -2 to 2
- ln1_gain: float32 [1024], replicated, may hold values from 0.5 to 1.5
- ln1_bias: float32 [1024], replicated, may hold values from -2 to 2
- w_qkv: bfloat16 [1024, 3, 1024], P(None, None, 'tensor'), may hold values from -0.1875 to 0.1875
- w_out: bfloat16 [1024, 1024], P('tensor'), may hold values from -0.5 to 0.5
- ln2_gain: float32 [1024], replicated, may hold values from 0.5 to 1.5
- ln2_bias: float32 [1024], replicated, may hold values from -2 to 2
- w_up: bfloat16 [1024, 4096], P(None, 'tensor'), may hold values from -0.1875 to 0.1875
- c_up: float32 [4096], P('tensor'), may hold values from -3 to 3
- w_down: bfloat16 [4096, 1024], P('tensor'), may hold values from -0.09375 to 0.09375
- cotangent: bfloat16 [16384, 1024], P(('section', 'dp')), may hold values from -6 to 6
Outputs:
- layer_out: float32 [16384, 1024], P(('section', 'dp', 'tensor'))
- d_decoder_in: float32 [16384, 1024], P(('section', 'dp'), 'tensor')
- d_encoder_out: bfloat16 [16384, 1024], P(('section', 'dp'), 'tensor')
- d_w_skip: float32 [2, 1024, 1024], P(None, 'tensor')
- d_b_skip: float32 [1024], replicated
- d_ln1_gain: float32 [1024], replicated
- d_ln1_bias: float32 [1024], replicated
- d_w_qkv: float32 [1024, 3, 1024], P(None, None, 'tensor')
- d_w_out: float32 [1024, 1024], P('tensor')
- d_ln2_gain: float32 [1024], replicated
- d_ln2_bias: float32 [1024], replicated
- d_w_up: float32 [1024, 4096], P(None, 'tensor')
- d_c_up: float32 [4096], P('tensor')
- d_w_down: float32 [4096, 1024], P('tensor')
Inputs may be any that keep to these rules, and one draw needn't show every extreme that they name: `segments`: along each packed row of 2048 frames the ids never fall; each utterance holds 1 to 1024 frames, and one of each row holds exactly 1024.
All inputs are finite; a program needn't handle non-finite values.
Results may differ from a plain program's by a relative error of at most 0.019.
Values may be sent and summed in bfloat16 or wider, within the bound.
No kernel may reach another device: no remote copies, remote signals or barrier semaphores. Data moves between devices by JAX's collectives and lax.ppermute only.
A program may use at most 192 MiB of HBM per device.

v0:
```python
import functools
import jax
import jax.numpy as jnp
from jax import lax
from jax.experimental import pallas as pl
from jax.experimental.pallas import tpu as pltpu
from jax.sharding import PartitionSpec as P

D = 1024
HEADS = 16
UTTS = 6
HEAD_DIM = D // HEADS
SCALE = HEAD_DIM**-0.5

EPSILON = 1e-05
FAR = 1e30
ROOT_HALF = 0.7071067811865476
INV_ROOT_TAU = 0.3989422804014327
BF16 = jnp.bfloat16
F32 = jnp.float32
NT = (((1,), (1,)), ((), ()))
NN = (((1,), (0,)), ((), ()))
TN = (((0,), (0,)), ((), ()))
CHUNKS = 2
PARTS = 4


def mm(left, right, dims):
    return lax.dot_general(left, right, dims, preferred_element_type=F32)


def starts_of(seg):
    return [jnp.sum((seg < u).astype(jnp.int32)) for u in range(1, UTTS)]


def tile_range(starts, first, count, tile, total):
    low = jnp.int32(0)
    high = jnp.int32(total)
    for s in starts:
        low = jnp.maximum(low, jnp.where(s <= first, s, 0))
        high = jnp.minimum(high, jnp.where(s >= first + count, s, total))
    return low // tile, (high + tile - 1) // tile


def eye(n):
    r = lax.broadcasted_iota(jnp.int32, (n, n), 0)
    c = lax.broadcasted_iota(jnp.int32, (n, n), 1)
    return jnp.where(r == c, 1.0, 0.0).astype(BF16)


def far_tile(starts, seg_row, q_first, k_first, bk, bq):
    kpos = k_first + lax.broadcasted_iota(jnp.int32, (bk, bq), 0)
    qpos = q_first + lax.broadcasted_iota(jnp.int32, (bk, bq), 1)
    lo = jnp.zeros_like(seg_row)
    hi = jnp.full_like(seg_row, starts[0])
    for u in range(1, UTTS):
        lo = jnp.where(seg_row == u, starts[u - 1], lo)
        hi = jnp.where(seg_row == u, starts[u] if u < UTTS - 1 else 1 << 30, hi)
    ok = (kpos >= lo) & (kpos < hi)
    return jnp.where(ok, jnp.abs(kpos - qpos).astype(F32), FAR)


def head_masked(pair, which):
    lane = lax.broadcasted_iota(jnp.int32, pair.shape, 1)
    keep = (lane < HEAD_DIM) if which == 0 else (lane >= HEAD_DIM)
    return jnp.where(keep, pair, 0.0).astype(BF16)


def load_pieces(core, pieces, whole_ref):
    rows = pieces[0].shape[1]
    for n, piece in enumerate(pieces):
        chunk, side = n // 2, n % 2
        for y in range(2):
            first = y * (4 * rows) + (core ^ side) * (2 * rows) + chunk * rows
            whole_ref[pl.ds(pl.multiple_of(first, rows), rows)] = piece[y]


def fwd_kernel(
    heads, bk, chunk, core_ref, slope_ref, seg_ref, w_ref, q00, q01, q10, q11, *refs
):
    out_ref, lse_ref, own_ref, *sib_refs = refs[-8 - PARTS : -5]
    qkv_ref, vt_ref, acc_ref, s_ref, top_ref = refs[-5:]
    strip = sib_refs[0].shape[0]
    total = seg_ref.shape[1]
    width = heads * HEAD_DIM
    bq = out_ref.shape[1] // 2
    core = core_ref[0]
    load_pieces(core, (q00, q01, q10, q11), qkv_ref)
    starts = starts_of(seg_ref[...])
    ident = eye(width)

    def prep(j, c):
        at = pl.ds(pl.multiple_of(j * bk, bk), bk)
        vt = mm(ident, qkv_ref[at, 2 * width : 3 * width], NT).astype(BF16)
        for h in range(heads):
            vt_ref[h * 80 : h * 80 + 64, at] = vt[h * 64 : (h + 1) * 64]
            vt_ref[h * 80 + 64 : (h + 1) * 80, at] = jnp.ones((16, bk), BF16)
        return c

    lax.fori_loop(0, total // bk, prep, 0)

    def q_step(i, c):
        side, y = i // 2, i % 2
        qi = pl.multiple_of(y * (4 * bq) + (core ^ side) * (2 * bq) + chunk * bq, bq)
        lo, hi = tile_range(starts, qi, bq, bk, total)
        seg_row = seg_ref[:, pl.ds(qi, bq)]
        acc_ref[...] = jnp.zeros_like(acc_ref)
        top_ref[...] = jnp.full_like(top_ref, -3e38)
        qs = []
        for h in range(heads):
            p = h // 2
            qp = qkv_ref[pl.ds(qi, bq), p * 128 : (p + 1) * 128].astype(F32) * SCALE
            qs.append(head_masked(qp, h % 2))

        def score_step(j, c):
            kj = pl.multiple_of(j * bk, bk)
            far = far_tile(starts, seg_row, qi, kj, bk, bq)
            for h in range(heads):
                p = h // 2
                kp = qkv_ref[pl.ds(kj, bk), width + p * 128 : width + (p + 1) * 128]
                s = mm(kp, qs[h], NT) - far * slope_ref[h]
                s_ref[h, pl.ds(kj, bk)] = s
                top_ref[h] = jnp.maximum(top_ref[h], jnp.max(s.reshape(bk // 8, 8, bq), axis=0))
            return c

        lax.fori_loop(lo, hi, score_step, 0)
        tops = [jnp.max(top_ref[h], axis=0, keepdims=True) for h in range(heads)]

        def mix_step(j, c):
            kj = pl.multiple_of(j * bk, bk)
            for h in range(heads):
                e = jnp.exp(s_ref[h, pl.ds(kj, bk)] - tops[h]).astype(BF16)
                hs = slice(h * 80, (h + 1) * 80)
                acc_ref[hs] = acc_ref[hs] + mm(vt_ref[hs, pl.ds(kj, bk)], e, NN)
            return c

        lax.fori_loop(lo, hi, mix_step, 0)
        outs = []
        for h in range(heads):
            whole = acc_ref[h * 80 + 64 : h * 80 + 65]
            outs.append((acc_ref[h * 80 : h * 80 + 64] * (1.0 / whole)).astype(BF16))
            lse_ref[i, h : h + 1] = tops[h] + jnp.log(whole)
        ot = jnp.concatenate(outs, axis=0)
        here = pl.ds(pl.multiple_of(y * bq, bq), bq)
        mixed = mm(eye(bq), ot, NT).astype(BF16)
        out_ref[side, here] = mixed
        part = mm(mixed, w_ref[...], NN).astype(BF16)

        @pl.when(side == 0)
        def _():
            own_ref[here] = part

        for n, sib_ref in enumerate(sib_refs):
            first = n * strip % bq

            @pl.when((side == 1) & (y == n * strip // bq))
            def _(sib_ref=sib_ref, first=first):
                sib_ref[...] = part[first : first + strip]

        return c

    lax.fori_loop(0, 4, q_step, 0)


def attend(chunk, core, slopes, seg, w_out, pieces, ahead=()):
    total = seg.shape[1]
    rows = pieces[0].shape[1]
    heads = pieces[0].shape[2] // (3 * HEAD_DIM)
    width = heads * HEAD_DIM
    bk = 256
    smem = pl.BlockSpec(memory_space=pltpu.SMEM)
    vmem = pl.BlockSpec(memory_space=pltpu.VMEM)
    hbm = pl.BlockSpec(memory_space=pl.ANY)
    return pl.pallas_call(
        functools.partial(fwd_kernel, heads, bk, chunk),
        out_shape=(
            jax.ShapeDtypeStruct((2, 2 * rows, width), BF16),
            jax.ShapeDtypeStruct((4, heads, rows), F32),
            jax.ShapeDtypeStruct((2 * rows, w_out.shape[1]), BF16),
        )
        + (jax.ShapeDtypeStruct((2 * rows // PARTS, w_out.shape[1]), BF16),) * PARTS,
        in_specs=[smem, smem] + [vmem] * 6 + [hbm] * len(ahead),
        out_specs=(vmem,) * (3 + PARTS),
        scratch_shapes=[
            pltpu.VMEM((total, 3 * width), BF16),
            pltpu.VMEM((heads * 80, total), BF16),
            pltpu.VMEM((heads * 80, rows), F32),
            pltpu.VMEM((heads, total, rows), F32),
            pltpu.VMEM((heads, 8, rows), F32),
        ],
        compiler_params=pltpu.CompilerParams(vmem_limit_bytes=28 << 20),
        name="attend",
    )(core, slopes, seg, w_out, *pieces, *ahead)


def bwd_kernel(heads, bk, chunk, *refs):
    core_ref, slope_ref, seg_ref, q00, q01, q10, q11, do0, do1, o_ref, lse_ref = refs[:11]
    if chunk == 0:
        dq_ref, dkv_ref = refs[-8:-6]
    else:
        dq_in, dkv_in = refs[11:13]
        dqkv_ref = refs[-7]
    qkv_ref, kt_ref, dqt_ref, dk_ref, dv_ref, delta_ref = refs[-6:]
    total = seg_ref.shape[1]
    width = heads * HEAD_DIM
    bq = o_ref.shape[1] // 2
    core = core_ref[0]
    load_pieces(core, (q00, q01, q10, q11), qkv_ref)
    starts = starts_of(seg_ref[...])
    ident = eye(width)
    hr = lax.broadcasted_iota(jnp.int32, (8, width), 0)
    hc = lax.broadcasted_iota(jnp.int32, (8, width), 1)
    pick = jnp.where(hr == hc // HEAD_DIM, 1.0, 0.0)

    def prep(j, c):
        at = pl.ds(pl.multiple_of(j * bk, bk), bk)
        kj = qkv_ref[at, width : 2 * width]
        kt_ref[:, at] = (mm(ident, kj, NT) * SCALE).astype(BF16)
        if chunk == 0:
            dk_ref[at] = jnp.zeros((bk, width), F32)
            dv_ref[at] = jnp.zeros((bk, width), F32)
        else:
            dk_ref[at] = dkv_in[at, :width]
            dv_ref[at] = dkv_in[at, width:]
        return c

    lax.fori_loop(0, total // bk, prep, 0)
    for side, do_ref in enumerate((do0, do1)):
        for y in range(2):
            at = slice(y * bq, (y + 1) * bq)
            prod = do_ref[at].astype(F32) * o_ref[side, at].astype(F32)
            delta_ref[side * 2 + y] = lax.dot_general(
                pick, prod, NT, precision=lax.Precision.HIGHEST, preferred_element_type=F32
            )

    for side, do_ref in enumerate((do0, do1)):

        def q_step(y, c, side=side, do_ref=do_ref):
            i = side * 2 + y
            qi = pl.multiple_of(y * (4 * bq) + (core ^ side) * (2 * bq) + chunk * bq, bq)
            here = pl.ds(pl.multiple_of(y * bq, bq), bq)
            lo, hi = tile_range(starts, qi, bq, bk, total)
            seg_row = seg_ref[:, pl.ds(qi, bq)]
            dqt_ref[...] = jnp.zeros_like(dqt_ref)
            qs, dos = [], []
            for h in range(heads):
                p = h // 2
                qp = qkv_ref[pl.ds(qi, bq), p * 128 : (p + 1) * 128].astype(F32) * SCALE
                qs.append(head_masked(qp, h % 2))
                dp = do_ref[here, p * 128 : (p + 1) * 128].astype(F32)
                dos.append(head_masked(dp, h % 2))
            lses = [lse_ref[i, h : h + 1] for h in range(heads)]
            deltas = [delta_ref[i, h : h + 1] for h in range(heads)]

            def k_step(j, c):
                kj = pl.multiple_of(j * bk, bk)
                at = pl.ds(kj, bk)
                far = far_tile(starts, seg_row, qi, kj, bk, bq)
                for p in range(heads // 2):
                    cols = slice(p * 128, (p + 1) * 128)
                    kp = qkv_ref[at, width + p * 128 : width + (p + 1) * 128]
                    vp = qkv_ref[at, 2 * width + p * 128 : 2 * width + (p + 1) * 128]
                    dv = dv_ref[at, cols]
                    dk = dk_ref[at, cols]
                    for h in (2 * p, 2 * p + 1):
                        s = mm(kp, qs[h], NT) - far * slope_ref[h]
                        w = jnp.exp(s - lses[h])
                        dw = mm(vp, dos[h], NT)
                        ds = (w * (dw - deltas[h])).astype(BF16)
                        dv = dv + mm(w.astype(BF16), dos[h], NN)
                        dk = dk + mm(ds, qs[h], NN)
                        hs = slice(h * HEAD_DIM, (h + 1) * HEAD_DIM)
                        dqt_ref[hs] = dqt_ref[hs] + mm(kt_ref[hs, at], ds, NN)
                    dv_ref[at, cols] = dv
                    dk_ref[at, cols] = dk
                return c

            lax.fori_loop(lo, hi, k_step, 0)
            dq = mm(eye(bq), dqt_ref[...].astype(BF16), NT).astype(BF16)
            if chunk == 0:
                dq_ref[side, here] = dq
            else:
                dqkv_ref[2 + side, here, :width] = dq
            return c

        lax.fori_loop(0, 2, q_step, 0)

    if chunk == 0:

        def finish(j, c):
            at = pl.ds(pl.multiple_of(j * bk, bk), bk)
            dkv_ref[at, :width] = dk_ref[at]
            dkv_ref[at, width:] = dv_ref[at]
            return c

        lax.fori_loop(0, total // bk, finish, 0)
    else:
        for side in range(2):
            dqkv_ref[side, :, :width] = dq_in[side]
        for n in range(4):
            part, side = n // 2, n % 2
            for y in range(2):
                first = y * (4 * bq) + (core ^ side) * (2 * bq) + part * bq
                at = pl.ds(pl.multiple_of(first, bq), bq)
                here = slice(y * bq, (y + 1) * bq)
                dqkv_ref[n, here, width : 2 * width] = dk_ref[at].astype(BF16)
                dqkv_ref[n, here, 2 * width :] = dv_ref[at].astype(BF16)


def attend_back(chunk, core, slopes, seg, pieces, d_heads, heads_out, lse, before=(), ahead=()):
    total = seg.shape[1]
    rows = pieces[0].shape[1]
    heads = pieces[0].shape[2] // (3 * HEAD_DIM)
    width = heads * HEAD_DIM
    bk = 256
    smem = pl.BlockSpec(memory_space=pltpu.SMEM)
    vmem = pl.BlockSpec(memory_space=pltpu.VMEM)
    hbm = pl.BlockSpec(memory_space=pl.ANY)
    if chunk == 0:
        out_shape = (
            jax.ShapeDtypeStruct((2, 2 * rows, width), BF16),
            jax.ShapeDtypeStruct((total, 2 * width), F32),
        )
        out_specs = (vmem, vmem)
    else:
        out_shape = jax.ShapeDtypeStruct((4, 2 * rows, 3 * width), BF16)
        out_specs = vmem
    return pl.pallas_call(
        functools.partial(bwd_kernel, heads, bk, chunk),
        out_shape=out_shape,
        in_specs=[smem, smem] + [vmem] * (9 + len(before)) + [hbm] * len(ahead),
        out_specs=out_specs,
        scratch_shapes=[
            pltpu.VMEM((total, 3 * width), BF16),
            pltpu.VMEM((width, total), BF16),
            pltpu.VMEM((width, rows), F32),
            pltpu.VMEM((total, width), F32),
            pltpu.VMEM((total, width), F32),
            pltpu.VMEM((4, 8, rows), F32),
        ],
        compiler_params=pltpu.CompilerParams(vmem_limit_bytes=34 << 20),
        name="attend_back",
    )(core, slopes, seg, *pieces, *d_heads, heads_out, lse, *before, *ahead)


def swap(value, axis, bit):
    pairs = [(source, source ^ (1 << bit)) for source in range(lax.axis_size(axis))]
    return lax.ppermute(value, axis, pairs)


core_swap = functools.partial(swap, axis="tensor", bit=0)
chip_swap = functools.partial(swap, axis="tensor", bit=1)
partner_swap = functools.partial(swap, axis="section", bit=0)


def add_low(*terms):
    return sum(term.astype(F32) for term in terms).astype(BF16)


def group_steps():
    steps = [("section", 0)]
    for bit in range((lax.axis_size("dp") - 1).bit_length()):
        steps.append(("dp", bit))
    return steps


def gate(values, *ahead):
    hbm = pl.BlockSpec(memory_space=pl.ANY)
    many = isinstance(values, (list, tuple))
    values = tuple(values) if many else (values,)
    out = pl.pallas_call(
        lambda *refs: None,
        out_shape=tuple(jax.ShapeDtypeStruct(value.shape, value.dtype) for value in values),
        in_specs=[hbm] * (len(values) + len(ahead)),
        out_specs=(hbm,) * len(values),
        input_output_aliases={n: n for n in range(len(values))},
        name="gate",
    )(*values, *ahead)
    return out if many else out[0]


def fold_kernel(halving, mine_ref, kept_ref, came_ref, *refs):
    total = (kept_ref[...].astype(F32) + came_ref[...].astype(F32)).astype(BF16)
    if halving:
        put_halves(mine_ref[0], total, *refs[-2:])
    else:
        refs[-1][...] = total


def put_halves(mine, total, kept_ref, sent_ref, half=None):
    rows = kept_ref.shape[0]
    for n in range(2) if half is None else (half,):
        part = total[n * rows : (n + 1) * rows] if half is None else total

        @pl.when(mine == n)
        def _(part=part):
            kept_ref[...] = part

        @pl.when(mine != n)
        def _(part=part):
            sent_ref[...] = part


def fold(kept, came, mine, ahead):
    rows, width = kept.shape
    vmem = pl.BlockSpec(memory_space=pltpu.VMEM)
    halving = mine is not None
    shape = jax.ShapeDtypeStruct((rows // 2 if halving else rows, width), BF16)
    scalar = mine if halving else jnp.int32(0)
    out = pl.pallas_call(
        functools.partial(fold_kernel, halving),
        out_shape=(shape,) * (2 if halving else 1),
        in_specs=[pl.BlockSpec(memory_space=pltpu.SMEM), vmem, vmem]
        + [pl.BlockSpec(memory_space=pl.ANY)] * len(ahead),
        out_specs=(vmem,) * (2 if halving else 1),
        compiler_params=pltpu.CompilerParams(vmem_limit_bytes=12 << 20),
        name="fold",
    )(scalar.reshape(1), kept, came, *ahead)
    return out if halving else (out[0], None)


def join_kernel(mine_ref, value_ref, came_ref, *refs):
    out_ref = refs[-1]
    rows = value_ref.shape[0]
    mine = mine_ref[0]
    out_ref[pl.ds(pl.multiple_of(mine * rows, rows), rows)] = value_ref[...]
    out_ref[pl.ds(pl.multiple_of((1 - mine) * rows, rows), rows)] = came_ref[...]


def join(value, came, mine, ahead):
    rows, width = value.shape
    if rows % 16:
        came = gate(came, *ahead) if ahead else came
        first = mine == 0
        return jnp.concatenate(
            [jnp.where(first, value, came), jnp.where(first, came, value)], axis=0
        )
    vmem = pl.BlockSpec(memory_space=pltpu.VMEM)
    return pl.pallas_call(
        join_kernel,
        out_shape=jax.ShapeDtypeStruct((2 * rows, width), BF16),
        in_specs=[pl.BlockSpec(memory_space=pltpu.SMEM), vmem, vmem]
        + [pl.BlockSpec(memory_space=pl.ANY)] * len(ahead),
        out_specs=vmem,
        compiler_params=pltpu.CompilerParams(vmem_limit_bytes=12 << 20),
        name="join",
    )(mine.reshape(1), value, came, *ahead)


class GroupSum:
    def __init__(self, kept, sent, steps, mines):
        self.steps, self.mines = steps, mines
        self.count, self.kept = 0, kept
        self.done = False
        self.came = swap(sent, *steps[0])

    def step(self, *ahead):
        levels = len(self.steps)
        self.count += 1
        if self.count <= levels:
            following = self.mines[self.count] if self.count < levels else None
            rows = self.kept.shape[0]
            if self.count < levels and rows % 32:
                came = gate(self.came, *ahead) if ahead else self.came
                halves = add_low(self.kept, came).reshape(2, rows // 2, -1)
                self.kept = lax.dynamic_index_in_dim(halves, following, 0, keepdims=False)
                sent = lax.dynamic_index_in_dim(halves, 1 - following, 0, keepdims=False)
            else:
                self.kept, sent = fold(self.kept, self.came, following, ahead)
            if self.count < levels:
                self.came = swap(sent, *self.steps[self.count])
        else:
            level = 2 * levels - self.count
            self.kept = join(self.kept, self.came, self.mines[level], ahead)
        if self.count == 2 * levels:
            self.done = True
        elif self.count >= levels:
            self.came = swap(self.kept, *self.steps[2 * levels - 1 - self.count])
        return self.kept


def grads_kernel(mine_ref, *refs):
    norms, d_qkv_ref, heads, d_rows = refs[:4], refs[4], refs[5:7], refs[7:11]
    kept_ref, sent_ref, held_ref = refs[-3:]
    width = d_qkv_ref.shape[2]
    strip = 256
    half = kept_ref.shape[0]
    for n in range(2):
        for first in range(0, half, strip):
            at = slice(n * half + first, n * half + first + strip)
            to = slice(first, first + strip)
            total = sum(mm(norms[k][:, at], d_qkv_ref[k], TN) for k in range(4))
            held_ref[to, :width] = total.astype(BF16)
            total = sum(mm(d_rows[k][:, at], heads[k // 2][k % 2], TN) for k in range(4))
            held_ref[to, width:] = total.astype(BF16)
        put_halves(mine_ref[0], held_ref[...], kept_ref, sent_ref, half=n)


def late_grads(mine, norms, d_qkv, heads_out, d_rows, ahead):
    depth = norms[0].shape[1]
    width = d_qkv.shape[2] + heads_out[0].shape[2]
    vmem = pl.BlockSpec(memory_space=pltpu.VMEM)
    shape = jax.ShapeDtypeStruct((depth // 2, width), BF16)
    return pl.pallas_call(
        grads_kernel,
        out_shape=(shape, shape),
        in_specs=[pl.BlockSpec(memory_space=pltpu.SMEM)]
        + [vmem] * 11
        + [pl.BlockSpec(memory_space=pl.ANY)] * len(ahead),
        out_specs=(vmem, vmem),
        scratch_shapes=[pltpu.VMEM((depth // 2, width), BF16)],
        compiler_params=pltpu.CompilerParams(vmem_limit_bytes=32 << 20),
        name="late_grads",
    )(mine.reshape(1), *norms, d_qkv, *heads_out, *d_rows, *ahead)


def row_stats(values):
    row_mean = jnp.mean(values, axis=-1, keepdims=True)
    centered = values - row_mean
    inv_std = lax.rsqrt(jnp.mean(centered * centered, axis=-1, keepdims=True) + EPSILON)
    return centered * inv_std, inv_std


def norm_kernel(base_ref, mine_ref, other_ref, gain_ref, shift_ref, *refs):
    value_ref, low_ref = refs[-2:]
    value = base_ref[...] + (mine_ref[...].astype(F32) + other_ref[...].astype(F32))
    value_ref[...] = value
    normed, _ = row_stats(value)
    low_ref[...] = (normed * gain_ref[...] + shift_ref[...]).astype(BF16)


def norm_rows(base, mine, other, gain, shift, ahead=(), tile=128):
    rows, width = mine.shape
    wide = pl.BlockSpec((tile, width), lambda i: (i, 0))
    one = pl.BlockSpec((1, width), lambda i: (0, 0))
    return pl.pallas_call(
        norm_kernel,
        grid=(rows // tile,),
        out_shape=(
            jax.ShapeDtypeStruct((rows, width), F32),
            jax.ShapeDtypeStruct((rows, width), BF16),
        ),
        in_specs=[wide if base.shape[0] == rows else one, wide, wide, one, one]
        + [pl.BlockSpec(memory_space=pl.ANY)] * len(ahead),
        out_specs=(wide, wide),
        compiler_params=pltpu.CompilerParams(vmem_limit_bytes=24 << 20),
        name="norm_rows",
    )(base, mine, other, gain[None], shift[None], *ahead)


def back_kernel(past_ref, value_ref, mine_ref, other_ref, gain_ref, sums_in, *refs):
    grad_ref, low_ref, sums_ref = refs[-3:]
    d_output = mine_ref[...].astype(F32) + other_ref[...].astype(F32)
    normed, inv_std = row_stats(value_ref[...])
    d_normed = d_output * gain_ref[...]
    grad = past_ref[...].astype(F32) + inv_std * (
        d_normed
        - jnp.mean(d_normed, axis=-1, keepdims=True)
        - normed * jnp.mean(d_normed * normed, axis=-1, keepdims=True)
    )
    grad_ref[...] = grad
    low_ref[...] = grad.astype(BF16)

    @pl.when(pl.program_id(0) == 0)
    def _():
        sums_ref[...] = sums_in[...]

    for n, terms in enumerate((d_output * normed, d_output, grad)):
        part = jnp.sum(terms.reshape(-1, 8, terms.shape[1]), axis=0)
        sums_ref[n] = sums_ref[n] + part


def norm_back_rows(past, value, mine, other, gain, sums, ahead=(), tile=128):
    rows, width = mine.shape
    wide = pl.BlockSpec((tile, width), lambda i: (i, 0))
    one = pl.BlockSpec((1, width), lambda i: (0, 0))
    kept = pl.BlockSpec((3, 8, width), lambda i: (0, 0, 0))
    return pl.pallas_call(
        back_kernel,
        grid=(rows // tile,),
        out_shape=(
            jax.ShapeDtypeStruct((rows, width), F32),
            jax.ShapeDtypeStruct((rows, width), BF16),
            jax.ShapeDtypeStruct((3, 8, width), F32),
        ),
        in_specs=[wide, wide, wide, wide, one, kept]
        + [pl.BlockSpec(memory_space=pl.ANY)] * len(ahead),
        out_specs=(wide, wide, kept),
        compiler_params=pltpu.CompilerParams(vmem_limit_bytes=24 << 20),
        name="norm_back",
    )(past, value, mine, other, gain[None], sums, *ahead)


def feed_kernel(chunk, core_ref, up_ref, bias_ref, down_ref, own_ref, sib_ref, cot_ref, *refs):
    act_ref, grads_ref, bias_out, dn_own, *dn_sib = refs[-8 - PARTS : -4]
    cot_v, d_pre_ref, bias_acc, sems = refs[-4:]
    rows = own_ref.shape[0] // 2
    core = core_ref[0]
    copies = []
    for i in range(4):
        side, y = i // 2, i % 2
        first = y * (4 * rows) + (core ^ side) * (2 * rows) + chunk * rows
        copy = pltpu.make_async_copy(
            cot_ref.at[pl.ds(pl.multiple_of(first, rows), rows)],
            cot_v.at[i * rows : (i + 1) * rows],
            sems.at[i],
        )
        copy.start()
        copies.append(copy)
    bias_acc[...] = refs[1][...] if chunk else jnp.zeros_like(bias_acc)
    for copy in copies:
        copy.wait()
    for side, n_ref in enumerate((own_ref, sib_ref)):
        for y in range(2):
            here = slice(y * rows, (y + 1) * rows)
            there = slice((side * 2 + y) * rows, (side * 2 + y + 1) * rows)
            pre = mm(n_ref[here], up_ref[...], NN) + bias_ref[...]
            d_act = mm(cot_v[there], down_ref[...], NT)
            cdf = 0.5 + 0.5 * lax.erf(pre * ROOT_HALF)
            act_ref[side, here] = (pre * cdf).astype(BF16)
            slope = cdf + pre * jnp.exp(-0.5 * pre * pre) * INV_ROOT_TAU
            d_pre = (d_act * slope).astype(BF16)
            d_pre_ref[there] = d_pre
            parts = d_pre.astype(F32).reshape(-1, 8, d_pre.shape[1])
            bias_acc[...] = bias_acc[...] + jnp.sum(parts, axis=0)
            d_norm = mm(d_pre, up_ref[...], NT).astype(BF16)
            if side == 0:
                dn_own[here] = d_norm
            else:
                strip = dn_sib[0].shape[0]
                for n in range(rows // strip):
                    dn_sib[y * rows // strip + n][...] = d_norm[n * strip : (n + 1) * strip]
    bias_out[...] = bias_acc[...]
    own_rows, sib_rows = slice(0, 2 * rows), slice(2 * rows, 4 * rows)
    units = act_ref.shape[2]
    strip = 256
    for first in range(0, units, strip):
        at = slice(first, first + strip)
        total = mm(act_ref[0, :, at], cot_v[own_rows], TN) + mm(
            act_ref[1, :, at], cot_v[sib_rows], TN
        )
        if chunk:
            total = total + refs[0][at]
        grads_ref[at] = total.astype(grads_ref.dtype)
    for first in range(0, own_ref.shape[1], strip):
        at, to = slice(first, first + strip), slice(units + first, units + first + strip)
        total = mm(own_ref[:, at], d_pre_ref[own_rows], TN) + mm(
            sib_ref[:, at], d_pre_ref[sib_rows], TN
        )
        if chunk:
            total = total + refs[0][to]
        grads_ref[to] = total.astype(grads_ref.dtype)


def feed(chunk, core, w_up, c_up, w_down, own, sib, cot, before=()):
    rows, width = own.shape
    units = w_up.shape[1]
    vmem = pl.BlockSpec(memory_space=pltpu.VMEM)
    return pl.pallas_call(
        functools.partial(feed_kernel, chunk),
        out_shape=(
            jax.ShapeDtypeStruct((2, rows, units), BF16),
            jax.ShapeDtypeStruct((units + width, width), BF16 if chunk else F32),
            jax.ShapeDtypeStruct((8, units), F32),
            jax.ShapeDtypeStruct((rows, width), BF16),
        )
        + (jax.ShapeDtypeStruct((rows // PARTS, width), BF16),) * PARTS,
        in_specs=[pl.BlockSpec(memory_space=pltpu.SMEM)]
        + [vmem] * 5
        + [pl.BlockSpec(memory_space=pl.ANY)]
        + [vmem] * len(before),
        out_specs=(vmem,) * (4 + PARTS),
        scratch_shapes=[
            pltpu.VMEM((2 * rows, width), BF16),
            pltpu.VMEM((2 * rows, units), BF16),
            pltpu.VMEM((8, units), F32),
            pltpu.SemaphoreType.DMA((4,)),
        ],
        compiler_params=pltpu.CompilerParams(vmem_limit_bytes=44 << 20),
        name="feed",
    )(core, w_up, c_up[None], w_down, own, sib, cot, *before)


def row_copies(core, chunk, rows, source, target, sems, reverse=False):
    copies = []
    for i in range(4):
        side, y = i // 2, i % 2
        first = y * (4 * rows) + (core ^ side) * (2 * rows) + chunk * rows
        whole = pl.ds(pl.multiple_of(first, rows), rows)
        here = slice(i * rows, (i + 1) * rows)
        if reverse:
            copy = pltpu.make_async_copy(source.at[here], target.at[whole], sems.at[i])
        else:
            copy = pltpu.make_async_copy(source.at[whole], target.at[here], sems.at[i])
        copy.start()
        copies.append(copy)
    return copies


def skip_grad_kernel(chunk, core_ref, own_ref, sib_ref, dec_ref, enc_ref, *refs):
    outs, (dec_v, enc_v, sems) = refs[2 * chunk : -3], refs[-3:]
    rows = own_ref.shape[0] // 2
    width, cols = dec_v.shape[1], own_ref.shape[1]
    copies = row_copies(core_ref[0], chunk, rows, dec_ref, dec_v, sems.at[0])
    for i in range(4):
        side, y = i // 2, i % 2
        first = (y * 2 + (core_ref[0] ^ side)) * rows
        copy = pltpu.make_async_copy(
            enc_ref.at[pl.ds(pl.multiple_of(first, rows), rows)],
            enc_v.at[i * rows : (i + 1) * rows],
            sems.at[1, i],
        )
        copy.start()
        copies.append(copy)
    for copy in copies:
        copy.wait()
    half = 2 * rows
    for n, part in enumerate((dec_v, enc_v)):
        at = slice(n * width, (n + 1) * width)
        total = mm(part[:half], own_ref[...], TN) + mm(part[half:], sib_ref[...], TN)
        if not chunk:
            outs[0][at] = total
            continue
        total = (total + refs[0][at]).astype(BF16)
        side = jnp.zeros((width, 128), BF16)
        if n == 0:
            small = refs[1]
            lines = [
                small[k : k + 1, j * 128 : (j + 1) * 128] for k in range(8) for j in range(cols // 128)
            ]
            spare = jnp.zeros((width - len(lines), 128), F32)
            side = jnp.concatenate(lines + [spare], axis=0).astype(BF16)
        put_halves(core_ref[1], jnp.concatenate([total, side], axis=1), *outs, half=n)


def skip_grad(chunk, core, own, sib, dec, enc, before=()):
    rows, cols = own.shape
    width = dec.shape[1]
    vmem = pl.BlockSpec(memory_space=pltpu.VMEM)
    hbm = pl.BlockSpec(memory_space=pl.ANY)
    half = jax.ShapeDtypeStruct((width, cols + 128), BF16)
    return pl.pallas_call(
        functools.partial(skip_grad_kernel, chunk),
        out_shape=(half, half) if chunk else (jax.ShapeDtypeStruct((2 * width, cols), F32),),
        in_specs=[pl.BlockSpec(memory_space=pltpu.SMEM), vmem, vmem, hbm, hbm]
        + [vmem] * len(before),
        out_specs=(vmem,) * (1 + chunk),
        scratch_shapes=[
            pltpu.VMEM((2 * rows, width), BF16),
            pltpu.VMEM((2 * rows, width), BF16),
            pltpu.SemaphoreType.DMA((2, 4)),
        ],
        compiler_params=pltpu.CompilerParams(vmem_limit_bytes=24 << 20),
        name="skip_grad",
    )(core, own, sib, dec, enc, *before)


def skip_back_kernel(chunk, core_ref, w_ref, own_ref, sib_ref, *refs):
    back_ref, whole_ref, held, sems = refs[-4:]
    rows = own_ref.shape[0] // 2
    for side, part in enumerate((own_ref, sib_ref)):
        at = slice(side * 2 * rows, (side + 1) * 2 * rows)
        back_ref[at] = mm(part[...], w_ref[1], NT).astype(BF16)
        held[at] = mm(part[...], w_ref[0], NT)
    for copy in row_copies(core_ref[0], chunk, rows, held, whole_ref, sems, reverse=True):
        copy.wait()


def skip_back(chunk, core, w_skip, own, sib, group_rows, before=(), ahead=()):
    rows = own.shape[0]
    width = w_skip.shape[1]
    vmem = pl.BlockSpec(memory_space=pltpu.VMEM)
    hbm = pl.BlockSpec(memory_space=pl.ANY)
    return pl.pallas_call(
        functools.partial(skip_back_kernel, chunk),
        out_shape=(
            jax.ShapeDtypeStruct((2 * rows, width), BF16),
            jax.ShapeDtypeStruct((group_rows, width), F32),
        ),
        in_specs=[pl.BlockSpec(memory_space=pltpu.SMEM), vmem, vmem, vmem]
        + [hbm] * (len(before) + len(ahead)),
        out_specs=(vmem, hbm),
        scratch_shapes=[pltpu.VMEM((2 * rows, width), F32), pltpu.SemaphoreType.DMA((4,))],
        input_output_aliases={4: 1} if before else {},
        compiler_params=pltpu.CompilerParams(vmem_limit_bytes=24 << 20),
        name="skip_back",
    )(core, w_skip, own, sib, *before, *ahead)


def restore_kernel(core_ref, *refs):
    out_ref = refs[-1]
    for chunk, part in enumerate(refs[:-1]):
        rows = part.shape[0] // 4
        for i in range(4):
            side, y = i // 2, i % 2
            first = y * (4 * rows) + (core_ref[0] ^ side) * (2 * rows) + chunk * rows
            out_ref[pl.ds(pl.multiple_of(first, rows), rows)] = part[i * rows : (i + 1) * rows]


def restore(core, parts):
    vmem = pl.BlockSpec(memory_space=pltpu.VMEM)
    rows, width = parts[0].shape
    return pl.pallas_call(
        restore_kernel,
        out_shape=jax.ShapeDtypeStruct((rows * len(parts), width), parts[0].dtype),
        in_specs=[pl.BlockSpec(memory_space=pltpu.SMEM)] + [vmem] * len(parts),
        out_specs=vmem,
        compiler_params=pltpu.CompilerParams(vmem_limit_bytes=12 << 20),
        name="restore",
    )(core, *parts)


def skip_kernel(chunk, core_ref, w_ref, dec_ref, enc_ref, own_ref, *refs):
    sib_refs, (dec_v, enc_v, sems) = refs[:PARTS], refs[PARTS:]
    rows = own_ref.shape[0] // 2
    copies = row_copies(core_ref[0], chunk, rows, dec_ref, dec_v, sems.at[0])
    for i in range(4):
        side, y = i // 2, i % 2
        first = (y * 2 + (core_ref[0] ^ side)) * rows
        copy = pltpu.make_async_copy(
            enc_ref.at[pl.ds(pl.multiple_of(first, rows), rows)],
            enc_v.at[i * rows : (i + 1) * rows],
            sems.at[1, i],
        )
        copy.start()
        copies.append(copy)
    for copy in copies:
        copy.wait()
    half = 2 * rows
    strip = half // PARTS
    for n, sib_ref in enumerate(sib_refs):
        at = slice(half + n * strip, half + (n + 1) * strip)
        sib_ref[...] = (mm(dec_v[at], w_ref[0], NN) + mm(enc_v[at], w_ref[1], NN)).astype(BF16)
    own_ref[...] = (mm(dec_v[:half], w_ref[0], NN) + mm(enc_v[:half], w_ref[1], NN)).astype(BF16)


def skip(chunk, core, w_skip, dec, enc):
    rows = enc.shape[0] // 2
    width, cols = w_skip.shape[1:]
    vmem = pl.BlockSpec(memory_space=pltpu.VMEM)
    hbm = pl.BlockSpec(memory_space=pl.ANY)
    return pl.pallas_call(
        functools.partial(skip_kernel, chunk),
        out_shape=(jax.ShapeDtypeStruct((rows, cols), BF16),)
        + (jax.ShapeDtypeStruct((rows // PARTS, cols), BF16),) * PARTS,
        in_specs=[pl.BlockSpec(memory_space=pltpu.SMEM), vmem, hbm, hbm],
        out_specs=(vmem,) * (1 + PARTS),
        scratch_shapes=[
            pltpu.VMEM((2 * rows, width), BF16),
            pltpu.VMEM((2 * rows, width), BF16),
            pltpu.SemaphoreType.DMA((2, 4)),
        ],
        compiler_params=pltpu.CompilerParams(vmem_limit_bytes=16 << 20),
        name="skip",
    )(core, w_skip, dec, enc)


def shards(
    decoder_in,
    encoder_out,
    segments,
    w_skip,
    b_skip,
    ln1_gain,
    ln1_bias,
    w_qkv,
    w_out,
    ln2_gain,
    ln2_bias,
    w_up,
    c_up,
    w_down,
    cotangent,
):
    group_rows = decoder_in.shape[0]
    tensor_rank = lax.axis_index("tensor")
    core = tensor_rank & 1
    chip = tensor_rank >> 1
    heads_here = HEADS // lax.axis_size("tensor")
    local_width = heads_here * HEAD_DIM
    block = group_rows // (4 * CHUNKS)
    qkv_matrix = w_qkv.reshape(D, 3 * local_width)
    steps = group_steps()
    mines = [((lax.axis_index(axis) >> bit) & 1).astype(jnp.int32) for axis, bit in steps]
    core_scalar = jnp.stack([core.astype(jnp.int32), mines[0]])
    slopes = jnp.exp2(
        -8.0
        * (tensor_rank * heads_here + jnp.arange(heads_here, dtype=jnp.int32) + 1).astype(F32)
        / HEADS
    )
    spots = [(chunk, side) for chunk in range(CHUNKS) for side in range(2)]

    def piece_of(array, chunk, side):
        width = array.shape[-1]
        parts = array.reshape(2, 2, CHUNKS, block, width)[:, :, chunk]
        return lax.dynamic_index_in_dim(parts, core ^ side, 1, keepdims=False).reshape(
            2 * block, width
        )

    cot = [piece_of(cotangent, chunk, 0) for chunk in range(CHUNKS)]
    encoder_parts = encoder_out.reshape(2, 2, CHUNKS, block, encoder_out.shape[1])
    partner = [
        partner_swap(encoder_parts[:, :, chunk].reshape(4 * block, -1)) for chunk in range(CHUNKS)
    ]

    def chip_total(half):
        sent = core_swap(half(1).astype(BF16))
        return (half(0) + sent.astype(F32)).astype(BF16)

    merged, norm_one, qkv = [], {}, {}
    sums = []
    for chunk in range(CHUNKS):
        own, *sib = skip(chunk, core_scalar, w_skip, decoder_in, partner[chunk])
        sums.append(add_low(own, jnp.concatenate([core_swap(part) for part in sib], axis=0)))
        if chunk + 1 < CHUNKS:
            partner[chunk + 1] = gate(partner[chunk + 1], sums[chunk])
    others = [chip_swap(part) for part in sums]
    ahead = (qkv_matrix, *sums)
    for chunk in range(CHUNKS):
        value, normal = norm_rows(
            b_skip[None], sums[chunk], others[chunk], ln1_gain, ln1_bias, ahead
        )
        merged.append(value)
        norm_one[chunk, 0] = normal
        norm_one[chunk, 1] = core_swap(normal)
        for side in range(2):
            qkv[chunk, side] = jnp.dot(
                norm_one[chunk, side], qkv_matrix, preferred_element_type=F32
            ).astype(BF16)
        ahead = (qkv[chunk, 0], qkv[chunk, 1], *cot)
    qkv_pieces = [qkv[spot].reshape(2, block, 3 * local_width) for spot in spots]

    heads_out, lse, sums = [], [], []
    for chunk in range(CHUNKS):
        mixed, log_total, own, *sib = attend(
            chunk, core_scalar, slopes, segments, w_out, qkv_pieces, sums
        )
        heads_out.append(mixed)
        lse.append(log_total)
        sums.append(add_low(own, jnp.concatenate([core_swap(part) for part in sib], axis=0)))
    others = [chip_swap(part) for part in sums]

    attended, activated, d_sums, d_others = [], [], [], []
    ahead = tuple(sums)
    grads = ()
    for chunk in range(CHUNKS):
        value, normal = norm_rows(
            merged[chunk], sums[chunk], others[chunk], ln2_gain, ln2_bias, ahead
        )
        attended.append(value)
        acts, weights_sum, bias_sum, own, *sib = feed(
            chunk, core_scalar, w_up, c_up, w_down, normal, core_swap(normal), cotangent, grads
        )
        grads = (weights_sum, bias_sum)
        activated.append(acts)
        sib = gate([core_swap(part) for part in sib], d_others[chunk - 1] if chunk else others[1])
        d_sums.append(add_low(own, jnp.concatenate(sib, axis=0)))
        d_others.append(chip_swap(d_sums[chunk]))
        ahead = (d_sums[chunk],)
    d_w_ff, c_up_sum = grads
    both = ("section", "dp")
    d_w_ff = lax.psum_scatter(
        gate(d_w_ff, d_sums[-1]), both, scatter_dimension=0, tiled=True
    )

    d_attended, d_attended_rows = [], {}
    sums_two = jnp.zeros((3, 8, D), F32)
    before = ()
    for chunk in range(CHUNKS):
        value, low, sums_two = norm_back_rows(
            cot[chunk], attended[chunk], d_sums[chunk], d_others[chunk], ln2_gain, sums_two,
            ahead,
        )
        d_attended.append(value)
        d_attended_rows[chunk, 0] = low
        d_attended_rows[chunk, 1] = core_swap(low)
        d_heads = [
            mm(d_attended_rows[chunk, side], w_out, NT).astype(BF16) for side in range(2)
        ]
        before = attend_back(
            chunk, core_scalar, slopes, segments, qkv_pieces, d_heads, heads_out[chunk],
            lse[chunk], before,
        )
        ahead = (before[0],)
    d_qkv = before

    sums = [
        chip_total(lambda side: mm(d_qkv[2 * chunk + side], qkv_matrix, NT))
        for chunk in range(CHUNKS)
    ]
    others = [chip_swap(part) for part in sums]
    kept, sent = late_grads(
        mines[0],
        [norm_one[spot] for spot in spots],
        d_qkv,
        heads_out,
        [d_attended_rows[spot] for spot in spots],
        sums,
    )
    late = GroupSum(kept, sent, steps, mines)
    activated = gate(activated, kept)
    down = [
        chip_total(
            lambda side: jnp.dot(activated[chunk][side], w_down, preferred_element_type=F32)
        )
        for chunk in range(CHUNKS)
    ]

    aways = [
        lax.dynamic_index_in_dim(part.reshape(2, block, D), 1 - chip, 0, keepdims=False)
        for part in down
    ]
    lows = []
    sums_one = jnp.zeros((3, 8, D), F32)
    ahead = (kept,)
    for chunk in range(CHUNKS):
        _, low, sums_one = norm_back_rows(
            d_attended[chunk], merged[chunk], sums[chunk], others[chunk], ln1_gain, sums_one, ahead
        )
        lows.append(low)
        if chunk == 0:
            ahead = (late.step(low, *aways),)
    d_w_ff = lax.all_gather(gate(d_w_ff, lows[0]), both, axis=0, tiled=True)
    sibs = [core_swap(low) for low in lows]
    small = jnp.sum(jnp.concatenate([sums_one, sums_two], axis=0), axis=1) * 0.5
    small = small + core_swap(small)
    small = small + chip_swap(small)
    small = jnp.concatenate([small, jnp.sum(c_up_sum, axis=0)[None]], axis=0)
    small = jnp.pad(small, ((0, 16 - small.shape[0]), (0, 0)))
    before = ()
    for chunk in range(CHUNKS):
        before = skip_grad(
            chunk, core_scalar, lows[chunk], sibs[chunk], decoder_in, partner[chunk],
            (*before, small) if chunk else (),
        )
    kept, sent = before
    last = GroupSum(kept, sent, steps, mines)
    d_encoder, before = [], ()
    for chunk in range(CHUNKS):
        returned, *before = skip_back(
            chunk, core_scalar, w_skip, lows[chunk], sibs[chunk], group_rows, before, (kept,)
        )
        d_encoder.append(returned)
    (d_decoder_in,) = before
    d_encoder_out = restore(core_scalar, [partner_swap(part) for part in d_encoder])
    last.step(*d_encoder)

    moved = [chip_swap(part) for part in gate(aways, lows[-1])]
    d_w_down, d_w_up = d_w_ff[: w_down.shape[0]].astype(F32), d_w_ff[w_down.shape[0] :].astype(F32)
    total = 2 * len(steps)
    while last.count < total - 1:
        if late.count < total - 1:
            late.step(last.kept)
        last.step()
    moved = gate(moved, last.kept)
    layer_out = []
    for chunk in range(CHUNKS):
        home, base = (
            lax.dynamic_index_in_dim(part.reshape(2, block, D), chip, 0, keepdims=False)
            for part in (down[chunk], attended[chunk])
        )
        layer_out.append(base + (home.astype(F32) + moved[chunk].astype(F32)))
    layer_out = jnp.concatenate(layer_out, axis=0)
    while not late.done:
        late.step(last.kept, d_w_down, d_w_up, layer_out)
    last.step(d_encoder_out)
    d_w_qkv = late.kept[:, : 3 * local_width].reshape(w_qkv.shape)
    d_w_out = late.kept[:, 3 * local_width :].T
    d_w_skip = last.kept[:, :D].reshape(w_skip.shape)
    small = last.kept[: 8 * D // 128, D:].astype(F32).reshape(8, D)
    return (
        layer_out,
        d_decoder_in,
        d_encoder_out,
        d_w_skip.astype(F32),
        small[2],
        small[0],
        small[1],
        d_w_qkv.astype(F32),
        d_w_out.astype(F32),
        small[3],
        small[4],
        d_w_up,
        small[6],
        d_w_down,
    )


def solution(mesh):
    return jax.shard_map(
        shards,
        mesh=mesh,
        in_specs=(
            P(("section", "dp"), "tensor"),
            P(("section", "dp"), "tensor"),
            P(("section", "dp"), None),
            P(None, "tensor", None),
            P(),
            P(),
            P(),
            P(None, None, "tensor"),
            P("tensor", None),
            P(),
            P(),
            P(None, "tensor"),
            P("tensor"),
            P("tensor", None),
            P(("section", "dp"), None),
        ),
        out_specs=(
            P(("section", "dp", "tensor"), None),
            P(("section", "dp"), "tensor"),
            P(("section", "dp"), "tensor"),
            P(None, "tensor", None),
            P(),
            P(),
            P(),
            P(None, None, "tensor"),
            P("tensor", None),
            P(),
            P(),
            P(None, "tensor"),
            P("tensor"),
            P("tensor", None),
        ),
        check_vma=False,
    )
```

profile of v0, /device:TPU:0, one launch (start us, length us, event | category | flops | bytes accessed | tf_op | source)
XLA Modules:
  0.0 503.5 jit_solution(4989053317036859783)
XLA Ops:
  12.5 11.8 %collective-permute-done.enc_ref = bf16[1024,256]{1,0:T(8,128)(2,1)S(1)} collective-permute-done((bf16[1024,256]{1,0:T(8,128)(2,1)S(1)}, bf16[1024,256]{1,0:T(8,128)(2,1)S(1)}, u32[]{:S(2)}, u32[]{:S(2)}) %collective-permute-start) | collective-permute-done | bytes 524320 | tf_op jit(solution)/shard_map/ppermute | solution.py:348
  32.6 10.1 %collective-permute-done.6.refs_0_ = bf16[1024,256]{1,0:T(8,128)(2,1)} collective-permute-done((bf16[1024,256]{1,0:T(8,128)(2,1)S(1)}, bf16[1024,256]{1,0:T(8,128)(2,1)}, u32[]{:S(2)}, u32[]{:S(2)}) %collective-permute-start.6) | collective-permute-done | bytes 524320 | tf_op jit(solution)/shard_map/ppermute | solution.py:348
  42.7 4.1 skip.3
  56.2 3.9 norm_rows.4
  72.7 14.3 %collective-permute-done.12.other_ref = bf16[512,1024]{1,0:T(8,128)(2,1)S(1)} collective-permute-done((bf16[512,1024]{1,0:T(8,128)(2,1)S(1)}, bf16[512,1024]{1,0:T(8,128)(2,1)S(1)}, u32[]{:S(2)}, u32[]{:S(2)}) %collective-permute-start.12) | collective-permute-done | bytes 1048608 | tf_op jit(solution)/shard_map/ppermute | solution.py:348
  94.7 17.4 %attend.2 = (bf16[2,512,256]{2,1,0:T(8,128)(2,1)S(1)}, f32[4,4,256]{2,1,0:T(4,128)S(1)}, bf16[512,1024]{1,0:T(8,128)(2,1)S(1)}, bf16[128,1024]{1,0:T(8,128)(2,1)...) custom-call(s32[2]{0:T(128)S(1)} %pad_add_fusion.core_ref.refs_0_, ...), custom_call_target="tpu_custom_call" | custom-call | tf_op jit(solution)/shard_map/attend/pallas_call | solution.py:174
  117.2 14.6 %attend.3 = (bf16[2,512,256]{2,1,0:T(8,128)(2,1)S(1)}, f32[4,4,256]{2,1,0:T(4,128)S(1)}, bf16[512,1024]{1,0:T(8,128)(2,1)S(1)}, bf16[128,1024]{1,0:T(8,128)(2,1)...) custom-call(s32[2]{0:T(128)S(1)} %pad_add_fusion.core_ref.refs_0_, ...), custom_call_target="tpu_custom_call" | custom-call | tf_op jit(solution)/shard_map/attend/pallas_call | solution.py:174
  135.8 5.2 %collective-permute-done.18.other_ref = bf16[512,1024]{1,0:T(8,128)(2,1)S(1)} collective-permute-done((bf16[512,1024]{1,0:T(8,128)(2,1)S(1)}, bf16[512,1024]{1,0:T(8,128)(2,1)S(1)}, u32[]{:S(2)}, u32[]{:S(2)}) %collective-permute-start.18) | collective-permute-done | bytes 1048608 | tf_op jit(solution)/shard_map/ppermute | solution.py:348
  144.8 18.5 %feed.2 = (bf16[2,512,1024]{2,1,0:T(8,128)(2,1)S(1)}, f32[2048,1024]{1,0:T(8,128)}, f32[8,1024]{1,0:T(8,128)S(1)}, bf16[512,1024]{1,0:T(8,128)(2,1)S(1)}, bf16[1...) custom-call(s32[2]{0:T(128)S(1)} %pad_add_fusion.core_ref.refs_0_, ...), custom_call_target="tpu_custom_call" | custom-call | tf_op jit(solution)/shard_map/feed/pallas_call | solution.py:659
  174.0 9.6 %norm_rows.7 = (f32[512,1024]{1,0:T(8,128)S(1)}, bf16[512,1024]{1,0:T(8,128)(2,1)S(1)}) custom-call(f32[512,1024]{1,0:T(8,128)S(1)} %copy-done.27, bf16[512,1024]{1,0:T(8,128)(2,1)S(1)} %copy-done.22, bf16[512,1024]{1,0:T(8,128)(2,1)S(1)} %copy-done.42, f32[1,1024]{1,0:T(1,128)S(1)} %bitcast.148, f32[1,1024]{1,0:T(1,128)S(1)} %bitcast.158, ...), custom_call_target="tpu_custom_call" | custom-call | tf_op jit(solution)/shard_map/norm_rows/pallas_call | solution.py:536
  187.6 19.6 %feed.3 = (bf16[2,512,1024]{2,1,0:T(8,128)(2,1)S(1)}, bf16[2048,1024]{1,0:T(8,128)(2,1)}, f32[8,1024]{1,0:T(8,128)S(1)}, bf16[512,1024]{1,0:T(8,128)(2,1)S(1)}, ...) custom-call(s32[2]{0:T(128)S(1)} %pad_add_fusion.core_ref.refs_0_, ...), custom_call_target="tpu_custom_call" | custom-call | tf_op jit(solution)/shard_map/feed/pallas_call | solution.py:659
  227.9 26.6 %attend_back.2 = (bf16[2,512,256]{2,1,0:T(8,128)(2,1)S(1)}, f32[2048,512]{1,0:T(8,128)S(1)}) custom-call(s32[2]{0:T(128)S(1)} %pad_add_fusion.core_ref.refs_0_, f32[4]{0:T(128)S(1)} %multiply_exponential_fusion.slope_ref.refs_1_, s32[1,2048]{1,0:T(1,128)S(1)} %copy-done.75, bf16[2,256,768]{2,1,0:T(8,128)(2,1)S(1)} %bitcast.123, ...), custom_call_target="tpu_custom_call" | custom-call | tf_op jit(solution)/shard_map/attend_back/pallas_call | solution.py:328
  260.1 22.5 %attend_back.3.refs_4_ = bf16[4,512,768]{2,1,0:T(8,128)(2,1)S(1)} custom-call(s32[2]{0:T(128)S(1)} %pad_add_fusion.core_ref.refs_0_, f32[4]{0:T(128)S(1)} %multiply_exponential_fusion.slope_ref.refs_1_, s32[1,2048]{1,0:T(1,128)S(1)} %copy-done.75, bf16[2,256,768]{2,1,0:T(8,128)(2,1)S(1)} %bitcast.124, bf16[2,256,768]{2,1,0:T(8,128)(2,1)S(1)} %bitcast.128, ...), custom_call_target="tpu_custom_call" | custom-call | tf_op jit(solution)/shard_map/attend_back/pallas_call | solution.py:328
  290.2 7.3 %late_grads.1 = (bf16[512,1024]{1,0:T(8,128)(2,1)S(1)}, bf16[512,1024]{1,0:T(8,128)(2,1)S(1)}) custom-call(s32[1]{0:T(128)} %bitcast.2.mine_ref, bf16[512,1024]{1,0:T(8,128)(2,1)} %get-tuple-element.115.refs_0_, bf16[512,1024]{1,0:T(8,128)(2,1)} %collective-permute-done.11.refs_1_, bf16[512,1024]{1,0:T(8,128)(2,1)} %get-tuple-element.116.refs_2_, ...), custom_call_target="tpu_custom_call" | custom-call | tf_op jit(solution)/shard_map/late_grads/pallas_call | solution.py:504
  298.5 14.2 %collective-permute-done.43.other_ref = bf16[512,1024]{1,0:T(8,128)(2,1)S(1)} collective-permute-done((bf16[512,1024]{1,0:T(8,128)(2,1)S(1)}, bf16[512,1024]{1,0:T(8,128)(2,1)S(1)}, u32[]{:S(2)}, u32[]{:S(2)}) %collective-permute-start.43) | collective-permute-done | bytes 1048608 | tf_op jit(solution)/shard_map/ppermute | solution.py:348
  318.5 3.6 convolution_convert_fusion.2
  326.7 3.7 add_convert_fusion
  334.3 22.9 %collective-permute-done.44.came_ref = bf16[512,1024]{1,0:T(8,128)(2,1)S(1)} collective-permute-done((bf16[512,1024]{1,0:T(8,128)(2,1)}, bf16[512,1024]{1,0:T(8,128)(2,1)S(1)}, u32[]{:S(2)}, u32[]{:S(2)}) %collective-permute-start.44) | collective-permute-done | bytes 1048608 | tf_op jit(solution)/shard_map/ppermute | solution.py:348
  370.1 4.0 skip_grad.2.refs_0_
  374.1 4.7 skip_grad.3
  379.3 3.5 skip_back.2
  382.8 3.5 skip_back.3
  386.4 7.1 %collective-permute-done.51.came_ref = bf16[256,1152]{1,0:T(8,128)(2,1)S(1)} collective-permute-done((bf16[256,1152]{1,0:T(8,128)(2,1)S(1)}, bf16[256,1152]{1,0:T(8,128)(2,1)S(1)}, u32[]{:S(2)}, u32[]{:S(2)}) %collective-permute-start.51) | collective-permute-done | bytes 589856 | tf_op jit(solution)/shard_map/ppermute | solution.py:348
  395.9 9.5 %collective-permute-done.52.came_ref = bf16[128,1152]{1,0:T(8,128)(2,1)S(1)} collective-permute-done((bf16[128,1152]{1,0:T(8,128)(2,1)S(1)}, bf16[128,1152]{1,0:T(8,128)(2,1)S(1)}, u32[]{:S(2)}, u32[]{:S(2)}) %collective-permute-start.52) | collective-permute-done | bytes 294944 | tf_op jit(solution)/shard_map/ppermute | solution.py:348
  408.1 6.8 %collective-permute-done.53.came_ref = bf16[64,1152]{1,0:T(8,128)(2,1)S(1)} collective-permute-done((bf16[64,1152]{1,0:T(8,128)(2,1)S(1)}, bf16[64,1152]{1,0:T(8,128)(2,1)S(1)}, u32[]{:S(2)}, u32[]{:S(2)}) %collective-permute-start.53) | collective-permute-done | bytes 147488 | tf_op jit(solution)/shard_map/ppermute | solution.py:348
  415.0 3.5 collective-permute-start.54
  422.2 8.5 %collective-permute-done.54.came_ref = bf16[64,1152]{1,0:T(8,128)(2,1)S(1)} collective-permute-done((bf16[64,1152]{1,0:T(8,128)(2,1)S(1)}, bf16[64,1152]{1,0:T(8,128)(2,1)S(1)}, u32[]{:S(2)}, u32[]{:S(2)}) %collective-permute-start.54) | collective-permute-done | bytes 147488 | tf_op jit(solution)/shard_map/ppermute | solution.py:348
  439.0 10.3 %collective-permute-done.61.came_ref = bf16[128,1024]{1,0:T(8,128)(2,1)S(1)} collective-permute-done((bf16[128,1024]{1,0:T(8,128)(2,1)S(1)}, bf16[128,1024]{1,0:T(8,128)(2,1)S(1)}, u32[]{:S(2)}, u32[]{:S(2)}) %collective-permute-start.61) | collective-permute-done | bytes 262176 | tf_op jit(solution)/shard_map/ppermute | solution.py:348
  454.2 6.0 %collective-permute-done.62.came_ref = bf16[256,1024]{1,0:T(8,128)(2,1)S(1)} collective-permute-done((bf16[256,1024]{1,0:T(8,128)(2,1)S(1)}, bf16[256,1024]{1,0:T(8,128)(2,1)S(1)}, u32[]{:S(2)}, u32[]{:S(2)}) %collective-permute-start.62) | collective-permute-done | bytes 524320 | tf_op jit(solution)/shard_map/ppermute | solution.py:348
  461.6 5.3 %collective-permute-done.58.came_ref = bf16[256,1152]{1,0:T(8,128)(2,1)} collective-permute-done((bf16[256,1152]{1,0:T(8,128)(2,1)}, bf16[256,1152]{1,0:T(8,128)(2,1)}, u32[]{:S(2)}, u32[]{:S(2)}) %collective-permute-start.58) | collective-permute-done | bytes 589856 | tf_op jit(solution)/shard_map/ppermute | solution.py:348
  473.9 12.2 %collective-permute-done.63.came_ref = bf16[512,1024]{1,0:T(8,128)(2,1)} collective-permute-done((bf16[512,1024]{1,0:T(8,128)(2,1)}, bf16[512,1024]{1,0:T(8,128)(2,1)}, u32[]{:S(2)}, u32[]{:S(2)}) %collective-permute-start.63) | collective-permute-done | bytes 1048608 | tf_op jit(solution)/shard_map/ppermute | solution.py:348
  491.5 3.6 copy.61
  (405 shorter events, 169.4 us)
Async XLA Ops:
  7.2 309.6 %reduce-scatter.2.cloned.1.call-start = ((), (), s32[]{:S(2)}) async-start(), calls=%async_computation.1 | async-start | bytes 4718592 | tf_op jit(solution)/shard_map/reduce_scatter | solution.py:962
  9.5 14.9 %collective-permute-start = (bf16[1024,256]{1,0:T(8,128)(2,1)S(1)}, bf16[1024,256]{1,0:T(8,128)(2,1)S(1)}, u32[]{:S(2)}, u32[]{:S(2)}) collective-permute-start(bf16[1024,256]{1,0:T(8,128)(2,1)S(1)} %bitcast.177), channel_id=1, source_target_pairs={{0,16},{16,0},{1,17},{17,1},{2,18},{18,2},{3,19},{19,3},{4,20},{20... | collective-permute-start | bytes 1572872 | tf_op jit(solution)/shard_map/ppermute | solution.py:348
  28.7 14.0 %collective-permute-start.6 = (bf16[1024,256]{1,0:T(8,128)(2,1)S(1)}, bf16[1024,256]{1,0:T(8,128)(2,1)}, u32[]{:S(2)}, u32[]{:S(2)}) collective-permute-start(bf16[1024,256]{1,0:T(8,128)(2,1)S(1)} %bitcast.176), channel_id=1, source_target_pairs={{0,16},{16,0},{1,17},{17,1},{2,18},{18,2},{3,19},{19,3},{4,20},{20... | collective-permute-start | bytes 1572872 | tf_op jit(solution)/shard_map/ppermute | solution.py:348
  30.9 25.3 %collective-permute-start.5 = (bf16[512,1024]{1,0:T(8,128)(2,1)S(1)}, bf16[512,1024]{1,0:T(8,128)(2,1)}, u32[]{:S(2)}, u32[]{:S(2)}) collective-permute-start(bf16[512,1024]{1,0:T(8,128)(2,1)S(1)} %add_convert_fusion.9.refs_1_.mine_ref), channel_id=1, source_target_pairs={{0,2},{1,3},{2,0},{3,1},{4,6},{5,7},{6,4},{7,5},{8,10},{9,11},{10,... | collective-permute-start | bytes 3145736 | tf_op jit(solution)/shard_map/ppermute | solution.py:348
  61.4 8.9 %collective-permute-start.11 = (bf16[512,1024]{1,0:T(8,128)(2,1)}, bf16[512,1024]{1,0:T(8,128)(2,1)}, u32[]{:S(2)}, u32[]{:S(2)}) collective-permute-start(bf16[512,1024]{1,0:T(8,128)(2,1)} %get-tuple-element.115.refs_0_), channel_id=1, source_target_pairs={{0,1},{1,0},{2,3},{3,2},{4,5},{5,4},{6,7},{7,6},{8,9},{9,8},{10,11... | collective-permute-start | bytes 3145736 | tf_op jit(solution)/shard_map/ppermute | solution.py:348
  61.4 25.6 %collective-permute-start.12 = (bf16[512,1024]{1,0:T(8,128)(2,1)S(1)}, bf16[512,1024]{1,0:T(8,128)(2,1)S(1)}, u32[]{:S(2)}, u32[]{:S(2)}) collective-permute-start(bf16[512,1024]{1,0:T(8,128)(2,1)S(1)} %add_convert_fusion.8.refs_2_.mine_ref), channel_id=1, source_target_pairs={{0,2},{1,3},{2,0},{3,1},{4,6},{5,7},{6,4},{7,5},{8,10},{9,11},{10,... | collective-permute-start | bytes 3145736 | tf_op jit(solution)/shard_map/ppermute | solution.py:348
  115.4 25.5 %collective-permute-start.18 = (bf16[512,1024]{1,0:T(8,128)(2,1)S(1)}, bf16[512,1024]{1,0:T(8,128)(2,1)S(1)}, u32[]{:S(2)}, u32[]{:S(2)}) collective-permute-start(bf16[512,1024]{1,0:T(8,128)(2,1)S(1)} %add_convert_fusion.7.refs_0_.mine_ref), channel_id=1, source_target_pairs={{0,2},{1,3},{2,0},{3,1},{4,6},{5,7},{6,4},{7,5},{8,10},{9,11},{10,... | collective-permute-start | bytes 3145736 | tf_op jit(solution)/shard_map/ppermute | solution.py:348
  142.2 25.6 %collective-permute-start.24 = (bf16[512,1024]{1,0:T(8,128)(2,1)S(1)}, bf16[512,1024]{1,0:T(8,128)(2,1)S(1)}, u32[]{:S(2)}, u32[]{:S(2)}) collective-permute-start(bf16[512,1024]{1,0:T(8,128)(2,1)S(1)} %add_convert_fusion.6.refs_1_.mine_ref), channel_id=1, source_target_pairs={{0,2},{1,3},{2,0},{3,1},{4,6},{5,7},{6,4},{7,5},{8,10},{9,11},{10,... | collective-permute-start | bytes 3145736 | tf_op jit(solution)/shard_map/ppermute | solution.py:348
  185.0 25.6 %collective-permute-start.34 = (bf16[512,1024]{1,0:T(8,128)(2,1)S(1)}, bf16[512,1024]{1,0:T(8,128)(2,1)S(1)}, u32[]{:S(2)}, u32[]{:S(2)}) collective-permute-start(bf16[512,1024]{1,0:T(8,128)(2,1)S(1)} %add_convert_fusion.5.refs_0_.mine_ref), channel_id=1, source_target_pairs={{0,2},{1,3},{2,0},{3,1},{4,6},{5,7},{6,4},{7,5},{8,10},{9,11},{10,... | collective-permute-start | bytes 3145736 | tf_op jit(solution)/shard_map/ppermute | solution.py:348
  215.6 255.0 %all-gather.2.cloned.1.call-start = ((), (), s32[]{:S(2)}) async-start(), calls=%async_computation.2 | async-start | bytes 4718592 | tf_op jit(solution)/shard_map/all_gather | solution.py:1023
  224.7 29.7 %collective-permute-start.35 = (bf16[512,1024]{1,0:T(8,128)(2,1)S(1)}, bf16[512,1024]{1,0:T(8,128)(2,1)S(1)}, u32[]{:S(2)}, u32[]{:S(2)}) collective-permute-start(bf16[512,1024]{1,0:T(8,128)(2,1)S(1)} %copy-done.4), channel_id=1, source_target_pairs={{0,2},{1,3},{2,0},{3,1},{4,6},{5,7},{6,4},{7,5},{8,10},{9,11},{10,... | collective-permute-start | bytes 3145736 | tf_op jit(solution)/shard_map/ppermute | solution.py:348
  287.3 25.3 %collective-permute-start.43 = (bf16[512,1024]{1,0:T(8,128)(2,1)S(1)}, bf16[512,1024]{1,0:T(8,128)(2,1)S(1)}, u32[]{:S(2)}, u32[]{:S(2)}) collective-permute-start(bf16[512,1024]{1,0:T(8,128)(2,1)S(1)} %add_convert_fusion.3.refs_11_.mine_ref), channel_id=1, source_target_pairs={{0,2},{1,3},{2,0},{3,1},{4,6},{5,7},{6,4},{7,5},{8,10},{9,11},{10,... | collective-permute-start | bytes 3145736 | tf_op jit(solution)/shard_map/ppermute | solution.py:348
  324.3 7.1 %collective-permute-start.40 = (bf16[512,1024]{1,0:T(8,128)(2,1)}, bf16[512,1024]{1,0:T(8,128)(2,1)}, u32[]{:S(2)}, u32[]{:S(2)}) collective-permute-start(bf16[512,1024]{1,0:T(8,128)(2,1)} %convolution_convert_fusion.3), channel_id=1, source_target_pairs={{0,1},{1,0},{2,3},{3,2},{4,5},{5,4},{6,7},{7,6},{8,9},{9,8},{10,11... | collective-permute-start | bytes 3145736 | tf_op jit(solution)/shard_map/ppermute | solution.py:348
  324.8 33.8 %collective-permute-start.42 = (bf16[512,1024]{1,0:T(8,128)(2,1)S(1)}, bf16[512,1024]{1,0:T(8,128)(2,1)S(1)}, u32[]{:S(2)}, u32[]{:S(2)}) collective-permute-start(bf16[512,1024]{1,0:T(8,128)(2,1)S(1)} %add_convert_fusion.2.refs_12_.mine_ref), channel_id=1, source_target_pairs={{0,2},{1,3},{2,0},{3,1},{4,6},{5,7},{6,4},{7,5},{8,10},{9,11},{10,... | collective-permute-start | bytes 3145736 | tf_op jit(solution)/shard_map/ppermute | solution.py:348
  326.6 30.6 %collective-permute-start.44 = (bf16[512,1024]{1,0:T(8,128)(2,1)}, bf16[512,1024]{1,0:T(8,128)(2,1)S(1)}, u32[]{:S(2)}, u32[]{:S(2)}) collective-permute-start(bf16[512,1024]{1,0:T(8,128)(2,1)} %copy-done.84), channel_id=1, source_target_pairs={{0,16},{16,0},{1,17},{17,1},{2,18},{18,2},{3,19},{19,3},{4,20},{20... | collective-permute-start | bytes 3145736 | tf_op jit(solution)/shard_map/ppermute | solution.py:348
  326.6 42.5 %collective-permute-start.48 = (bf16[512,1024]{1,0:T(8,128)(2,1)S(1)}, bf16[512,1024]{1,0:T(8,128)(2,1)}, u32[]{:S(2)}, u32[]{:S(2)}) collective-permute-start(bf16[512,1024]{1,0:T(8,128)(2,1)S(1)} %copy-done.6), channel_id=1, source_target_pairs={{0,1},{1,0},{2,3},{3,2},{4,5},{5,4},{6,7},{7,6},{8,9},{9,8},{10,11... | collective-permute-start | bytes 3145736 | tf_op jit(solution)/shard_map/ppermute | solution.py:348
  362.3 11.7 %collective-permute-start.47 = (bf16[512,1024]{1,0:T(8,128)(2,1)S(1)}, bf16[512,1024]{1,0:T(8,128)(2,1)}, u32[]{:S(2)}, u32[]{:S(2)}) collective-permute-start(bf16[512,1024]{1,0:T(8,128)(2,1)S(1)} %get-tuple-element.172.refs_2_.own_ref), channel_id=1, source_target_pairs={{0,1},{1,0},{2,3},{3,2},{4,5},{5,4},{6,7},{7,6},{8,9},{9,8},{10,11... | collective-permute-start | bytes 3145736 | tf_op jit(solution)/shard_map/ppermute | solution.py:348
  378.8 14.6 %collective-permute-start.51 = (bf16[256,1152]{1,0:T(8,128)(2,1)S(1)}, bf16[256,1152]{1,0:T(8,128)(2,1)S(1)}, u32[]{:S(2)}, u32[]{:S(2)}) collective-permute-start(bf16[256,1152]{1,0:T(8,128)(2,1)S(1)} %get-tuple-element.179), channel_id=1, source_target_pairs={{0,16},{16,0},{1,17},{17,1},{2,18},{18,2},{3,19},{19,3},{4,20},{20... | collective-permute-start | bytes 1769480 | tf_op jit(solution)/shard_map/ppermute | solution.py:348
  393.8 11.6 %collective-permute-start.52 = (bf16[128,1152]{1,0:T(8,128)(2,1)S(1)}, bf16[128,1152]{1,0:T(8,128)(2,1)S(1)}, u32[]{:S(2)}, u32[]{:S(2)}) collective-permute-start(bf16[128,1152]{1,0:T(8,128)(2,1)S(1)} %get-tuple-element.184), channel_id=1, source_target_pairs={{0,4},{4,0},{8,12},{12,8},{1,5},{5,1},{9,13},{13,9},{2,6},{6,2},{1... | collective-permute-start | bytes 884744 | tf_op jit(solution)/shard_map/ppermute | solution.py:348
  395.7 22.7 %collective-permute-start.59 = (bf16[256,1024]{1,0:T(8,128)(2,1)S(1)}, bf16[256,1024]{1,0:T(8,128)(2,1)S(1)}, u32[]{:S(2)}, u32[]{:S(2)}) collective-permute-start(bf16[256,1024]{1,0:T(8,128)(2,1)S(1)} %copy-done.86), channel_id=1, source_target_pairs={{0,4},{4,0},{8,12},{12,8},{1,5},{5,1},{9,13},{13,9},{2,6},{6,2},{1... | collective-permute-start | bytes 1572872 | tf_op jit(solution)/shard_map/ppermute | solution.py:348
  405.7 9.2 %collective-permute-start.53 = (bf16[64,1152]{1,0:T(8,128)(2,1)S(1)}, bf16[64,1152]{1,0:T(8,128)(2,1)S(1)}, u32[]{:S(2)}, u32[]{:S(2)}) collective-permute-start(bf16[64,1152]{1,0:T(8,128)(2,1)S(1)} %get-tuple-element.186), channel_id=1, source_target_pairs={{0,8},{4,12},{8,0},{12,4},{1,9},{5,13},{9,1},{13,5},{2,10},{6,14},... | collective-permute-start | bytes 442376 | tf_op jit(solution)/shard_map/ppermute | solution.py:348
  407.4 27.9 %collective-permute-start.57 = (bf16[1024,256]{1,0:T(8,128)(2,1)}, bf16[1024,256]{1,0:T(8,128)(2,1)S(1)}, u32[]{:S(2)}, u32[]{:S(2)}) collective-permute-start(bf16[1024,256]{1,0:T(8,128)(2,1)} %copy-done.70), channel_id=1, source_target_pairs={{0,16},{16,0},{1,17},{17,1},{2,18},{18,2},{3,19},{19,3},{4,20},{20... | collective-permute-start | bytes 1572872 | tf_op jit(solution)/shard_map/ppermute | solution.py:348
  415.0 15.7 %collective-permute-start.54 = (bf16[64,1152]{1,0:T(8,128)(2,1)S(1)}, bf16[64,1152]{1,0:T(8,128)(2,1)S(1)}, u32[]{:S(2)}, u32[]{:S(2)}) collective-permute-start(bf16[64,1152]{1,0:T(8,128)(2,1)S(1)} %fold.9.value_ref.refs_0_), channel_id=1, source_target_pairs={{0,8},{4,12},{8,0},{12,4},{1,9},{5,13},{9,1},{13,5},{2,10},{6,14},... | collective-permute-start | bytes 442376 | tf_op jit(solution)/shard_map/ppermute | solution.py:348
  420.1 15.1 %collective-permute-start.60 = (bf16[128,1024]{1,0:T(8,128)(2,1)}, bf16[128,1024]{1,0:T(8,128)(2,1)S(1)}, u32[]{:S(2)}, u32[]{:S(2)}) collective-permute-start(bf16[128,1024]{1,0:T(8,128)(2,1)} %get-tuple-element.192), channel_id=1, source_target_pairs={{0,8},{4,12},{8,0},{12,4},{1,9},{5,13},{9,1},{13,5},{2,10},{6,14},... | collective-permute-start | bytes 786440 | tf_op jit(solution)/shard_map/ppermute | solution.py:348
  420.1 17.3 %collective-permute-start.56 = (bf16[1024,256]{1,0:T(8,128)(2,1)S(1)}, bf16[1024,256]{1,0:T(8,128)(2,1)S(1)}, u32[]{:S(2)}, u32[]{:S(2)}) collective-permute-start(bf16[1024,256]{1,0:T(8,128)(2,1)S(1)} %get-tuple-element.180.refs_0_), channel_id=1, source_target_pairs={{0,16},{16,0},{1,17},{17,1},{2,18},{18,2},{3,19},{19,3},{4,20},{20... | collective-permute-start | bytes 1572872 | tf_op jit(solution)/shard_map/ppermute | solution.py:348
  420.8 29.9 %collective-permute-start.45 = (bf16[256,1024]{1,0:T(8,128)(2,1)}, bf16[256,1024]{1,0:T(8,128)(2,1)}, u32[]{:S(2)}, u32[]{:S(2)}) collective-permute-start(bf16[256,1024]{1,0:T(8,128)(2,1)} %get-tuple-element.173), channel_id=1, source_target_pairs={{0,2},{1,3},{2,0},{3,1},{4,6},{5,7},{6,4},{7,5},{8,10},{9,11},{10,... | collective-permute-start | bytes 1572872 | tf_op jit(solution)/shard_map/ppermute | solution.py:348
  431.3 19.4 %collective-permute-start.46 = (bf16[256,1024]{1,0:T(8,128)(2,1)}, bf16[256,1024]{1,0:T(8,128)(2,1)}, u32[]{:S(2)}, u32[]{:S(2)}) collective-permute-start(bf16[256,1024]{1,0:T(8,128)(2,1)} %get-tuple-element.174), channel_id=1, source_target_pairs={{0,2},{1,3},{2,0},{3,1},{4,6},{5,7},{6,4},{7,5},{8,10},{9,11},{10,... | collective-permute-start | bytes 1572872 | tf_op jit(solution)/shard_map/ppermute | solution.py:348
  435.2 14.2 %collective-permute-start.55 = (bf16[128,1152]{1,0:T(8,128)(2,1)S(1)}, bf16[128,1152]{1,0:T(8,128)(2,1)S(1)}, u32[]{:S(2)}, u32[]{:S(2)}) collective-permute-start(bf16[128,1152]{1,0:T(8,128)(2,1)S(1)} %join.6.value_ref.refs_0_), channel_id=1, source_target_pairs={{0,4},{4,0},{8,12},{12,8},{1,5},{5,1},{9,13},{13,9},{2,6},{6,2},{1... | collective-permute-start | bytes 884744 | tf_op jit(solution)/shard_map/ppermute | solution.py:348
  435.3 14.0 %collective-permute-start.61 = (bf16[128,1024]{1,0:T(8,128)(2,1)S(1)}, bf16[128,1024]{1,0:T(8,128)(2,1)S(1)}, u32[]{:S(2)}, u32[]{:S(2)}) collective-permute-start(bf16[128,1024]{1,0:T(8,128)(2,1)S(1)} %fold.11.value_ref), channel_id=1, source_target_pairs={{0,8},{4,12},{8,0},{12,4},{1,9},{5,13},{9,1},{13,5},{2,10},{6,14},... | collective-permute-start | bytes 786440 | tf_op jit(solution)/shard_map/ppermute | solution.py:348
  449.4 10.8 %collective-permute-start.62 = (bf16[256,1024]{1,0:T(8,128)(2,1)S(1)}, bf16[256,1024]{1,0:T(8,128)(2,1)S(1)}, u32[]{:S(2)}, u32[]{:S(2)}) collective-permute-start(bf16[256,1024]{1,0:T(8,128)(2,1)S(1)} %join.9.value_ref), channel_id=1, source_target_pairs={{0,4},{4,0},{8,12},{12,8},{1,5},{5,1},{9,13},{13,9},{2,6},{6,2},{1... | collective-permute-start | bytes 1572872 | tf_op jit(solution)/shard_map/ppermute | solution.py:348
  450.4 16.6 %collective-permute-start.58 = (bf16[256,1152]{1,0:T(8,128)(2,1)}, bf16[256,1152]{1,0:T(8,128)(2,1)}, u32[]{:S(2)}, u32[]{:S(2)}) collective-permute-start(bf16[256,1152]{1,0:T(8,128)(2,1)} %join.7.refs_2_.value_ref.refs_0_), channel_id=1, source_target_pairs={{0,16},{16,0},{1,17},{17,1},{2,18},{18,2},{3,19},{19,3},{4,20},{20... | collective-permute-start | bytes 1769480 | tf_op jit(solution)/shard_map/ppermute | solution.py:348
  461.3 24.9 %collective-permute-start.63 = (bf16[512,1024]{1,0:T(8,128)(2,1)}, bf16[512,1024]{1,0:T(8,128)(2,1)}, u32[]{:S(2)}, u32[]{:S(2)}) collective-permute-start(bf16[512,1024]{1,0:T(8,128)(2,1)} %join.10.value_ref), channel_id=1, source_target_pairs={{0,16},{16,0},{1,17},{17,1},{2,18},{18,2},{3,19},{19,3},{4,20},{20... | collective-permute-start | bytes 3145736 | tf_op jit(solution)/shard_map/ppermute | solution.py:348
  (139 other events, 885.3 us)
Sparse Core Ops, SparseCore 0:
  215.8 87.6 reduce-scatter.1
  317.0 78.0 all-gather.1
where the time goes:
time: 511 us; the launch traced here: 504 us
  Pallas kernels  186 us (36%)
  waiting for transfers between devices  165 us (32%)
  local copies, waits for them, and re-layouts  49.3 us (10%)
  starting transfers between devices  41.9 us (8%)
  matrix products  27.4 us (5%)
  other arithmetic  17.6 us (3%)
  between operations  15.7 us (3%)
    ppermute x64, waiting for transfers between devices, swap(): return lax.ppermute(value, axis, pairs)  165 us
    pallas_call x2, Pallas kernels, attend_back(): pl.pallas_call(functools.partial(bwd_kernel, heads, bk, chunk), out_shape...  49.1 us
    ppermute x64, starting transfers between devices, swap(): return lax.ppermute(value, axis, pairs)  41.8 us
    unnamed x213, local copies, waits for them, and re-layouts  39.3 us
    pallas_call x2, Pallas kernels, feed(): pl.pallas_call(functools.partial(feed_kernel, chunk), out_shape=(jax.Shap...  38.2 us
    pallas_call x2, Pallas kernels, attend(): pl.pallas_call(functools.partial(fwd_kernel, heads, bk, chunk), out_shape...  32 us
    pallas_call x4, Pallas kernels, norm_rows(): pl.pallas_call(norm_kernel, grid=(rows // tile,), out_shape=(jax.ShapeDty...  16.8 us
    dot_general x4, matrix products, shards(): jnp.dot(activated[chunk][side], w_down, preferred_element_type=F32)  12.3 us
  transfers between devices with their start and end apart: 66, of which 33 were waited for; matrix products, arithmetic and copies ran while one was open for 9% of the time, Pallas kernels for 29%

commit v1 on v0

--- a/solution.py
+++ b/solution.py
@@ -1064,7 +1064,10 @@
     while not late.done:
         late.step(last.kept, d_w_down, d_w_up, layer_out)
     last.step(d_encoder_out)
-    d_w_qkv = late.kept[:, : 3 * local_width].reshape(w_qkv.shape)
+    d_w_qkv = jnp.stack(
+        [late.kept[:, n * local_width : (n + 1) * local_width] for n in range(3)], axis=0
+    )
+    d_w_qkv = jnp.transpose(d_w_qkv.astype(F32), (1, 0, 2))
     d_w_out = late.kept[:, 3 * local_width :].T
     d_w_skip = last.kept[:, :D].reshape(w_skip.shape)
     small = last.kept[: 8 * D // 128, D:].astype(F32).reshape(8, D)

time: 511 us -> 504 us (0.986)
  local copies, waits for them, and re-layouts: 49.3 us -> 44.1 us
    unnamed x213 -> x210, local copies, waits for them, and re-layouts: 39.3 us -> 36.5 us
  transfers between devices with their start and end apart: 66 -> 66, of which waited for: 33 -> 34; matrix products, arithmetic and copies ran while one was open for 9% -> 9% of each run, Pallas kernels for 29% -> 30%
where the time goes in v1:
time: 504 us; the launch traced here: 499 us
  Pallas kernels  186 us (37%)
  waiting for transfers between devices  163 us (32%)
  local copies, waits for them, and re-layouts  44.1 us (9%)
  starting transfers between devices  43.9 us (9%)
  matrix products  27.4 us (5%)
  other arithmetic  18.4 us (4%)
  between operations  15.7 us (3%)
    ppermute x64, waiting for transfers between devices, swap(): return lax.ppermute(value, axis, pairs)  163 us
    pallas_call x2, Pallas kernels, attend_back(): pl.pallas_call(functools.partial(bwd_kernel, heads, bk, chunk), out_shape...  49.1 us
    ppermute x64, starting transfers between devices, swap(): return lax.ppermute(value, axis, pairs)  43.8 us
    pallas_call x2, Pallas kernels, feed(): pl.pallas_call(functools.partial(feed_kernel, chunk), out_shape=(jax.Shap...  38.2 us
    unnamed x210, local copies, waits for them, and re-layouts  36.5 us
    pallas_call x2, Pallas kernels, attend(): pl.pallas_call(functools.partial(fwd_kernel, heads, bk, chunk), out_shape...  32 us
    pallas_call x4, Pallas kernels, norm_rows(): pl.pallas_call(norm_kernel, grid=(rows // tile,), out_shape=(jax.ShapeDty...  16.8 us
    dot_general x4, matrix products, shards(): jnp.dot(activated[chunk][side], w_down, preferred_element_type=F32)  12.3 us
  transfers between devices with their start and end apart: 66, of which 34 were waited for; matrix products, arithmetic and copies ran while one was open for 9% of the time, Pallas kernels for 30%

profile of v1, /device:TPU:0, one launch (start us, length us, event | category | flops | bytes accessed | tf_op | source)
XLA Modules:
  0.0 498.8 jit_solution(15279409308482676915)
XLA Ops:
  12.5 11.8 %collective-permute-done.enc_ref = bf16[1024,256]{1,0:T(8,128)(2,1)S(1)} collective-permute-done((bf16[1024,256]{1,0:T(8,128)(2,1)S(1)}, bf16[1024,256]{1,0:T(8,128)(2,1)S(1)}, u32[]{:S(2)}, u32[]{:S(2)}) %collective-permute-start) | collective-permute-done | bytes 524320 | tf_op jit(solution)/shard_map/ppermute | solution.py:348
  32.6 10.1 %collective-permute-done.6.refs_0_ = bf16[1024,256]{1,0:T(8,128)(2,1)} collective-permute-done((bf16[1024,256]{1,0:T(8,128)(2,1)S(1)}, bf16[1024,256]{1,0:T(8,128)(2,1)}, u32[]{:S(2)}, u32[]{:S(2)}) %collective-permute-start.6) | collective-permute-done | bytes 524320 | tf_op jit(solution)/shard_map/ppermute | solution.py:348
  42.7 4.1 skip.3
  56.2 3.9 norm_rows.4
  72.7 14.3 %collective-permute-done.12.other_ref = bf16[512,1024]{1,0:T(8,128)(2,1)S(1)} collective-permute-done((bf16[512,1024]{1,0:T(8,128)(2,1)S(1)}, bf16[512,1024]{1,0:T(8,128)(2,1)S(1)}, u32[]{:S(2)}, u32[]{:S(2)}) %collective-permute-start.12) | collective-permute-done | bytes 1048608 | tf_op jit(solution)/shard_map/ppermute | solution.py:348
  94.7 14.9 %attend.2 = (bf16[2,512,256]{2,1,0:T(8,128)(2,1)S(1)}, f32[4,4,256]{2,1,0:T(4,128)S(1)}, bf16[512,1024]{1,0:T(8,128)(2,1)S(1)}, bf16[128,1024]{1,0:T(8,128)(2,1)...) custom-call(s32[2]{0:T(128)S(1)} %pad_add_fusion.core_ref.refs_0_, ...), custom_call_target="tpu_custom_call" | custom-call | tf_op jit(solution)/shard_map/attend/pallas_call | solution.py:174
  114.7 17.1 %attend.3 = (bf16[2,512,256]{2,1,0:T(8,128)(2,1)S(1)}, f32[4,4,256]{2,1,0:T(4,128)S(1)}, bf16[512,1024]{1,0:T(8,128)(2,1)S(1)}, bf16[128,1024]{1,0:T(8,128)(2,1)...) custom-call(s32[2]{0:T(128)S(1)} %pad_add_fusion.core_ref.refs_0_, ...), custom_call_target="tpu_custom_call" | custom-call | tf_op jit(solution)/shard_map/attend/pallas_call | solution.py:174
  142.3 18.6 %feed.2 = (bf16[2,512,1024]{2,1,0:T(8,128)(2,1)S(1)}, f32[2048,1024]{1,0:T(8,128)}, f32[8,1024]{1,0:T(8,128)S(1)}, bf16[512,1024]{1,0:T(8,128)(2,1)S(1)}, bf16[1...) custom-call(s32[2]{0:T(128)S(1)} %pad_add_fusion.core_ref.refs_0_, ...), custom_call_target="tpu_custom_call" | custom-call | tf_op jit(solution)/shard_map/feed/pallas_call | solution.py:659
  171.5 9.6 %norm_rows.7 = (f32[512,1024]{1,0:T(8,128)S(1)}, bf16[512,1024]{1,0:T(8,128)(2,1)S(1)}) custom-call(f32[512,1024]{1,0:T(8,128)S(1)} %copy-done.27, bf16[512,1024]{1,0:T(8,128)(2,1)S(1)} %copy-done.22, bf16[512,1024]{1,0:T(8,128)(2,1)S(1)} %copy-done.42, f32[1,1024]{1,0:T(1,128)S(1)} %bitcast.155, f32[1,1024]{1,0:T(1,128)S(1)} %bitcast.165, ...), custom_call_target="tpu_custom_call" | custom-call | tf_op jit(solution)/shard_map/norm_rows/pallas_call | solution.py:536
  185.1 19.7 %feed.3 = (bf16[2,512,1024]{2,1,0:T(8,128)(2,1)S(1)}, bf16[2048,1024]{1,0:T(8,128)(2,1)}, f32[8,1024]{1,0:T(8,128)S(1)}, bf16[512,1024]{1,0:T(8,128)(2,1)S(1)}, ...) custom-call(s32[2]{0:T(128)S(1)} %pad_add_fusion.core_ref.refs_0_, ...), custom_call_target="tpu_custom_call" | custom-call | tf_op jit(solution)/shard_map/feed/pallas_call | solution.py:659
  225.4 22.1 %attend_back.2 = (bf16[2,512,256]{2,1,0:T(8,128)(2,1)S(1)}, f32[2048,512]{1,0:T(8,128)S(1)}) custom-call(s32[2]{0:T(128)S(1)} %pad_add_fusion.core_ref.refs_0_, f32[4]{0:T(128)S(1)} %multiply_exponential_fusion.slope_ref.refs_1_, s32[1,2048]{1,0:T(1,128)S(1)} %copy-done.75, bf16[2,256,768]{2,1,0:T(8,128)(2,1)S(1)} %bitcast.130, ...), custom_call_target="tpu_custom_call" | custom-call | tf_op jit(solution)/shard_map/attend_back/pallas_call | solution.py:328
  253.4 27.0 %attend_back.3.refs_4_ = bf16[4,512,768]{2,1,0:T(8,128)(2,1)S(1)} custom-call(s32[2]{0:T(128)S(1)} %pad_add_fusion.core_ref.refs_0_, f32[4]{0:T(128)S(1)} %multiply_exponential_fusion.slope_ref.refs_1_, s32[1,2048]{1,0:T(1,128)S(1)} %copy-done.75, bf16[2,256,768]{2,1,0:T(8,128)(2,1)S(1)} %bitcast.131, bf16[2,256,768]{2,1,0:T(8,128)(2,1)S(1)} %bitcast.135, ...), custom_call_target="tpu_custom_call" | custom-call | tf_op jit(solution)/shard_map/attend_back/pallas_call | solution.py:328
  287.9 7.3 %late_grads.1 = (bf16[512,1024]{1,0:T(8,128)(2,1)S(1)}, bf16[512,1024]{1,0:T(8,128)(2,1)S(1)}) custom-call(s32[1]{0:T(128)} %bitcast.2.mine_ref, bf16[512,1024]{1,0:T(8,128)(2,1)} %get-tuple-element.115.refs_0_, bf16[512,1024]{1,0:T(8,128)(2,1)} %collective-permute-done.11.refs_1_, bf16[512,1024]{1,0:T(8,128)(2,1)} %get-tuple-element.116.refs_2_, ...), custom_call_target="tpu_custom_call" | custom-call | tf_op jit(solution)/shard_map/late_grads/pallas_call | solution.py:504
  296.2 14.2 %collective-permute-done.43.other_ref = bf16[512,1024]{1,0:T(8,128)(2,1)S(1)} collective-permute-done((bf16[512,1024]{1,0:T(8,128)(2,1)S(1)}, bf16[512,1024]{1,0:T(8,128)(2,1)S(1)}, u32[]{:S(2)}, u32[]{:S(2)}) %collective-permute-start.43) | collective-permute-done | bytes 1048608 | tf_op jit(solution)/shard_map/ppermute | solution.py:348
  316.2 3.6 convolution_convert_fusion.2
  324.4 3.8 add_convert_fusion
  332.0 22.9 %collective-permute-done.44.came_ref = bf16[512,1024]{1,0:T(8,128)(2,1)S(1)} collective-permute-done((bf16[512,1024]{1,0:T(8,128)(2,1)}, bf16[512,1024]{1,0:T(8,128)(2,1)S(1)}, u32[]{:S(2)}, u32[]{:S(2)}) %collective-permute-start.44) | collective-permute-done | bytes 1048608 | tf_op jit(solution)/shard_map/ppermute | solution.py:348
  363.4 3.9 collective-permute-done.50
  368.4 4.0 skip_grad.2.refs_0_
  372.4 4.7 skip_grad.3
  377.2 3.5 skip_back.2
  380.8 3.5 skip_back.3
  384.3 8.4 %collective-permute-done.51.came_ref = bf16[256,1152]{1,0:T(8,128)(2,1)S(1)} collective-permute-done((bf16[256,1152]{1,0:T(8,128)(2,1)S(1)}, bf16[256,1152]{1,0:T(8,128)(2,1)S(1)}, u32[]{:S(2)}, u32[]{:S(2)}) %collective-permute-start.51) | collective-permute-done | bytes 589856 | tf_op jit(solution)/shard_map/ppermute | solution.py:348
  395.1 7.9 %collective-permute-done.52.came_ref = bf16[128,1152]{1,0:T(8,128)(2,1)S(1)} collective-permute-done((bf16[128,1152]{1,0:T(8,128)(2,1)S(1)}, bf16[128,1152]{1,0:T(8,128)(2,1)S(1)}, u32[]{:S(2)}, u32[]{:S(2)}) %collective-permute-start.52) | collective-permute-done | bytes 294944 | tf_op jit(solution)/shard_map/ppermute | solution.py:348
  403.4 4.1 collective-permute-start.53
  408.2 6.8 %collective-permute-done.53.came_ref = bf16[64,1152]{1,0:T(8,128)(2,1)S(1)} collective-permute-done((bf16[64,1152]{1,0:T(8,128)(2,1)S(1)}, bf16[64,1152]{1,0:T(8,128)(2,1)S(1)}, u32[]{:S(2)}, u32[]{:S(2)}) %collective-permute-start.53) | collective-permute-done | bytes 147488 | tf_op jit(solution)/shard_map/ppermute | solution.py:348
  415.0 3.5 collective-permute-start.54
  422.4 8.5 %collective-permute-done.54.came_ref = bf16[64,1152]{1,0:T(8,128)(2,1)S(1)} collective-permute-done((bf16[64,1152]{1,0:T(8,128)(2,1)S(1)}, bf16[64,1152]{1,0:T(8,128)(2,1)S(1)}, u32[]{:S(2)}, u32[]{:S(2)}) %collective-permute-start.54) | collective-permute-done | bytes 147488 | tf_op jit(solution)/shard_map/ppermute | solution.py:348
  439.8 9.9 %collective-permute-done.61.came_ref = bf16[128,1024]{1,0:T(8,128)(2,1)S(1)} collective-permute-done((bf16[128,1024]{1,0:T(8,128)(2,1)S(1)}, bf16[128,1024]{1,0:T(8,128)(2,1)S(1)}, u32[]{:S(2)}, u32[]{:S(2)}) %collective-permute-start.61) | collective-permute-done | bytes 262176 | tf_op jit(solution)/shard_map/ppermute | solution.py:348
  454.5 6.0 %collective-permute-done.62.came_ref = bf16[256,1024]{1,0:T(8,128)(2,1)S(1)} collective-permute-done((bf16[256,1024]{1,0:T(8,128)(2,1)S(1)}, bf16[256,1024]{1,0:T(8,128)(2,1)S(1)}, u32[]{:S(2)}, u32[]{:S(2)}) %collective-permute-start.62) | collective-permute-done | bytes 524320 | tf_op jit(solution)/shard_map/ppermute | solution.py:348
  461.7 5.7 %collective-permute-done.58.came_ref = bf16[256,1152]{1,0:T(8,128)(2,1)} collective-permute-done((bf16[256,1152]{1,0:T(8,128)(2,1)}, bf16[256,1152]{1,0:T(8,128)(2,1)}, u32[]{:S(2)}, u32[]{:S(2)}) %collective-permute-start.58) | collective-permute-done | bytes 589856 | tf_op jit(solution)/shard_map/ppermute | solution.py:348
  474.3 12.3 %collective-permute-done.63.came_ref = bf16[512,1024]{1,0:T(8,128)(2,1)} collective-permute-done((bf16[512,1024]{1,0:T(8,128)(2,1)}, bf16[512,1024]{1,0:T(8,128)(2,1)}, u32[]{:S(2)}, u32[]{:S(2)}) %collective-permute-start.63) | collective-permute-done | bytes 1048608 | tf_op jit(solution)/shard_map/ppermute | solution.py:348
  (401 shorter events, 165.7 us)
Async XLA Ops:
  7.2 307.4 %reduce-scatter.2.cloned.1.call-start = ((), (), s32[]{:S(2)}) async-start(), calls=%async_computation.1 | async-start | bytes 4718592 | tf_op jit(solution)/shard_map/reduce_scatter | solution.py:962
  9.5 14.9 %collective-permute-start = (bf16[1024,256]{1,0:T(8,128)(2,1)S(1)}, bf16[1024,256]{1,0:T(8,128)(2,1)S(1)}, u32[]{:S(2)}, u32[]{:S(2)}) collective-permute-start(bf16[1024,256]{1,0:T(8,128)(2,1)S(1)} %bitcast.183), channel_id=1, source_target_pairs={{0,16},{16,0},{1,17},{17,1},{2,18},{18,2},{3,19},{19,3},{4,20},{20... | collective-permute-start | bytes 1572872 | tf_op jit(solution)/shard_map/ppermute | solution.py:348
  28.7 14.0 %collective-permute-start.6 = (bf16[1024,256]{1,0:T(8,128)(2,1)S(1)}, bf16[1024,256]{1,0:T(8,128)(2,1)}, u32[]{:S(2)}, u32[]{:S(2)}) collective-permute-start(bf16[1024,256]{1,0:T(8,128)(2,1)S(1)} %bitcast.182), channel_id=1, source_target_pairs={{0,16},{16,0},{1,17},{17,1},{2,18},{18,2},{3,19},{19,3},{4,20},{20... | collective-permute-start | bytes 1572872 | tf_op jit(solution)/shard_map/ppermute | solution.py:348
  30.9 25.3 %collective-permute-start.5 = (bf16[512,1024]{1,0:T(8,128)(2,1)S(1)}, bf16[512,1024]{1,0:T(8,128)(2,1)}, u32[]{:S(2)}, u32[]{:S(2)}) collective-permute-start(bf16[512,1024]{1,0:T(8,128)(2,1)S(1)} %add_convert_fusion.9.refs_1_.mine_ref), channel_id=1, source_target_pairs={{0,2},{1,3},{2,0},{3,1},{4,6},{5,7},{6,4},{7,5},{8,10},{9,11},{10,... | collective-permute-start | bytes 3145736 | tf_op jit(solution)/shard_map/ppermute | solution.py:348
  61.4 8.9 %collective-permute-start.11 = (bf16[512,1024]{1,0:T(8,128)(2,1)}, bf16[512,1024]{1,0:T(8,128)(2,1)}, u32[]{:S(2)}, u32[]{:S(2)}) collective-permute-start(bf16[512,1024]{1,0:T(8,128)(2,1)} %get-tuple-element.115.refs_0_), channel_id=1, source_target_pairs={{0,1},{1,0},{2,3},{3,2},{4,5},{5,4},{6,7},{7,6},{8,9},{9,8},{10,11... | collective-permute-start | bytes 3145736 | tf_op jit(solution)/shard_map/ppermute | solution.py:348
  61.4 25.6 %collective-permute-start.12 = (bf16[512,1024]{1,0:T(8,128)(2,1)S(1)}, bf16[512,1024]{1,0:T(8,128)(2,1)S(1)}, u32[]{:S(2)}, u32[]{:S(2)}) collective-permute-start(bf16[512,1024]{1,0:T(8,128)(2,1)S(1)} %add_convert_fusion.8.refs_2_.mine_ref), channel_id=1, source_target_pairs={{0,2},{1,3},{2,0},{3,1},{4,6},{5,7},{6,4},{7,5},{8,10},{9,11},{10,... | collective-permute-start | bytes 3145736 | tf_op jit(solution)/shard_map/ppermute | solution.py:348
  112.9 25.5 %collective-permute-start.18 = (bf16[512,1024]{1,0:T(8,128)(2,1)S(1)}, bf16[512,1024]{1,0:T(8,128)(2,1)S(1)}, u32[]{:S(2)}, u32[]{:S(2)}) collective-permute-start(bf16[512,1024]{1,0:T(8,128)(2,1)S(1)} %add_convert_fusion.7.refs_0_.mine_ref), channel_id=1, source_target_pairs={{0,2},{1,3},{2,0},{3,1},{4,6},{5,7},{6,4},{7,5},{8,10},{9,11},{10,... | collective-permute-start | bytes 3145736 | tf_op jit(solution)/shard_map/ppermute | solution.py:348
  139.7 25.6 %collective-permute-start.24 = (bf16[512,1024]{1,0:T(8,128)(2,1)S(1)}, bf16[512,1024]{1,0:T(8,128)(2,1)S(1)}, u32[]{:S(2)}, u32[]{:S(2)}) collective-permute-start(bf16[512,1024]{1,0:T(8,128)(2,1)S(1)} %add_convert_fusion.6.refs_1_.mine_ref), channel_id=1, source_target_pairs={{0,2},{1,3},{2,0},{3,1},{4,6},{5,7},{6,4},{7,5},{8,10},{9,11},{10,... | collective-permute-start | bytes 3145736 | tf_op jit(solution)/shard_map/ppermute | solution.py:348
  182.4 25.6 %collective-permute-start.34 = (bf16[512,1024]{1,0:T(8,128)(2,1)S(1)}, bf16[512,1024]{1,0:T(8,128)(2,1)S(1)}, u32[]{:S(2)}, u32[]{:S(2)}) collective-permute-start(bf16[512,1024]{1,0:T(8,128)(2,1)S(1)} %add_convert_fusion.5.refs_0_.mine_ref), channel_id=1, source_target_pairs={{0,2},{1,3},{2,0},{3,1},{4,6},{5,7},{6,4},{7,5},{8,10},{9,11},{10,... | collective-permute-start | bytes 3145736 | tf_op jit(solution)/shard_map/ppermute | solution.py:348
  213.1 257.9 %all-gather.2.cloned.1.call-start = ((), (), s32[]{:S(2)}) async-start(), calls=%async_computation.2 | async-start | bytes 4718592 | tf_op jit(solution)/shard_map/all_gather | solution.py:1023
  222.2 25.6 %collective-permute-start.35 = (bf16[512,1024]{1,0:T(8,128)(2,1)S(1)}, bf16[512,1024]{1,0:T(8,128)(2,1)S(1)}, u32[]{:S(2)}, u32[]{:S(2)}) collective-permute-start(bf16[512,1024]{1,0:T(8,128)(2,1)S(1)} %copy-done.4), channel_id=1, source_target_pairs={{0,2},{1,3},{2,0},{3,1},{4,6},{5,7},{6,4},{7,5},{8,10},{9,11},{10,... | collective-permute-start | bytes 3145736 | tf_op jit(solution)/shard_map/ppermute | solution.py:348
  285.1 25.3 %collective-permute-start.43 = (bf16[512,1024]{1,0:T(8,128)(2,1)S(1)}, bf16[512,1024]{1,0:T(8,128)(2,1)S(1)}, u32[]{:S(2)}, u32[]{:S(2)}) collective-permute-start(bf16[512,1024]{1,0:T(8,128)(2,1)S(1)} %add_convert_fusion.3.refs_11_.mine_ref), channel_id=1, source_target_pairs={{0,2},{1,3},{2,0},{3,1},{4,6},{5,7},{6,4},{7,5},{8,10},{9,11},{10,... | collective-permute-start | bytes 3145736 | tf_op jit(solution)/shard_map/ppermute | solution.py:348
  322.0 7.2 %collective-permute-start.40 = (bf16[512,1024]{1,0:T(8,128)(2,1)}, bf16[512,1024]{1,0:T(8,128)(2,1)}, u32[]{:S(2)}, u32[]{:S(2)}) collective-permute-start(bf16[512,1024]{1,0:T(8,128)(2,1)} %convolution_convert_fusion.3), channel_id=1, source_target_pairs={{0,1},{1,0},{2,3},{3,2},{4,5},{5,4},{6,7},{7,6},{8,9},{9,8},{10,11... | collective-permute-start | bytes 3145736 | tf_op jit(solution)/shard_map/ppermute | solution.py:348
  322.5 33.8 %collective-permute-start.42 = (bf16[512,1024]{1,0:T(8,128)(2,1)S(1)}, bf16[512,1024]{1,0:T(8,128)(2,1)S(1)}, u32[]{:S(2)}, u32[]{:S(2)}) collective-permute-start(bf16[512,1024]{1,0:T(8,128)(2,1)S(1)} %add_convert_fusion.2.refs_12_.mine_ref), channel_id=1, source_target_pairs={{0,2},{1,3},{2,0},{3,1},{4,6},{5,7},{6,4},{7,5},{8,10},{9,11},{10,... | collective-permute-start | bytes 3145736 | tf_op jit(solution)/shard_map/ppermute | solution.py:348
  324.3 30.6 %collective-permute-start.44 = (bf16[512,1024]{1,0:T(8,128)(2,1)}, bf16[512,1024]{1,0:T(8,128)(2,1)S(1)}, u32[]{:S(2)}, u32[]{:S(2)}) collective-permute-start(bf16[512,1024]{1,0:T(8,128)(2,1)} %copy-done.84), channel_id=1, source_target_pairs={{0,16},{16,0},{1,17},{17,1},{2,18},{18,2},{3,19},{19,3},{4,20},{20... | collective-permute-start | bytes 3145736 | tf_op jit(solution)/shard_map/ppermute | solution.py:348
  324.3 43.1 %collective-permute-start.48 = (bf16[512,1024]{1,0:T(8,128)(2,1)S(1)}, bf16[512,1024]{1,0:T(8,128)(2,1)}, u32[]{:S(2)}, u32[]{:S(2)}) collective-permute-start(bf16[512,1024]{1,0:T(8,128)(2,1)S(1)} %copy-done.6), channel_id=1, source_target_pairs={{0,1},{1,0},{2,3},{3,2},{4,5},{5,4},{6,7},{7,6},{8,9},{9,8},{10,11... | collective-permute-start | bytes 3145736 | tf_op jit(solution)/shard_map/ppermute | solution.py:348
  360.6 11.7 %collective-permute-start.47 = (bf16[512,1024]{1,0:T(8,128)(2,1)S(1)}, bf16[512,1024]{1,0:T(8,128)(2,1)}, u32[]{:S(2)}, u32[]{:S(2)}) collective-permute-start(bf16[512,1024]{1,0:T(8,128)(2,1)S(1)} %get-tuple-element.172.refs_2_.own_ref), channel_id=1, source_target_pairs={{0,1},{1,0},{2,3},{3,2},{4,5},{5,4},{6,7},{7,6},{8,9},{9,8},{10,11... | collective-permute-start | bytes 3145736 | tf_op jit(solution)/shard_map/ppermute | solution.py:348
  377.1 15.6 %collective-permute-start.51 = (bf16[256,1152]{1,0:T(8,128)(2,1)S(1)}, bf16[256,1152]{1,0:T(8,128)(2,1)S(1)}, u32[]{:S(2)}, u32[]{:S(2)}) collective-permute-start(bf16[256,1152]{1,0:T(8,128)(2,1)S(1)} %get-tuple-element.179), channel_id=1, source_target_pairs={{0,16},{16,0},{1,17},{17,1},{2,18},{18,2},{3,19},{19,3},{4,20},{20... | collective-permute-start | bytes 1769480 | tf_op jit(solution)/shard_map/ppermute | solution.py:348
  393.0 10.0 %collective-permute-start.52 = (bf16[128,1152]{1,0:T(8,128)(2,1)S(1)}, bf16[128,1152]{1,0:T(8,128)(2,1)S(1)}, u32[]{:S(2)}, u32[]{:S(2)}) collective-permute-start(bf16[128,1152]{1,0:T(8,128)(2,1)S(1)} %get-tuple-element.184), channel_id=1, source_target_pairs={{0,4},{4,0},{8,12},{12,8},{1,5},{5,1},{9,13},{13,9},{2,6},{6,2},{1... | collective-permute-start | bytes 884744 | tf_op jit(solution)/shard_map/ppermute | solution.py:348
  394.5 24.0 %collective-permute-start.59 = (bf16[256,1024]{1,0:T(8,128)(2,1)S(1)}, bf16[256,1024]{1,0:T(8,128)(2,1)S(1)}, u32[]{:S(2)}, u32[]{:S(2)}) collective-permute-start(bf16[256,1024]{1,0:T(8,128)(2,1)S(1)} %copy-done.86), channel_id=1, source_target_pairs={{0,4},{4,0},{8,12},{12,8},{1,5},{5,1},{9,13},{13,9},{2,6},{6,2},{1... | collective-permute-start | bytes 1572872 | tf_op jit(solution)/shard_map/ppermute | solution.py:348
  403.4 11.6 %collective-permute-start.53 = (bf16[64,1152]{1,0:T(8,128)(2,1)S(1)}, bf16[64,1152]{1,0:T(8,128)(2,1)S(1)}, u32[]{:S(2)}, u32[]{:S(2)}) collective-permute-start(bf16[64,1152]{1,0:T(8,128)(2,1)S(1)} %get-tuple-element.186), channel_id=1, source_target_pairs={{0,8},{4,12},{8,0},{12,4},{1,9},{5,13},{9,1},{13,5},{2,10},{6,14},... | collective-permute-start | bytes 442376 | tf_op jit(solution)/shard_map/ppermute | solution.py:348
  407.5 28.2 %collective-permute-start.57 = (bf16[1024,256]{1,0:T(8,128)(2,1)}, bf16[1024,256]{1,0:T(8,128)(2,1)S(1)}, u32[]{:S(2)}, u32[]{:S(2)}) collective-permute-start(bf16[1024,256]{1,0:T(8,128)(2,1)} %copy-done.70), channel_id=1, source_target_pairs={{0,16},{16,0},{1,17},{17,1},{2,18},{18,2},{3,19},{19,3},{4,20},{20... | collective-permute-start | bytes 1572872 | tf_op jit(solution)/shard_map/ppermute | solution.py:348
  415.0 15.9 %collective-permute-start.54 = (bf16[64,1152]{1,0:T(8,128)(2,1)S(1)}, bf16[64,1152]{1,0:T(8,128)(2,1)S(1)}, u32[]{:S(2)}, u32[]{:S(2)}) collective-permute-start(bf16[64,1152]{1,0:T(8,128)(2,1)S(1)} %fold.9.value_ref.refs_0_), channel_id=1, source_target_pairs={{0,8},{4,12},{8,0},{12,4},{1,9},{5,13},{9,1},{13,5},{2,10},{6,14},... | collective-permute-start | bytes 442376 | tf_op jit(solution)/shard_map/ppermute | solution.py:348
  420.2 15.4 %collective-permute-start.60 = (bf16[128,1024]{1,0:T(8,128)(2,1)}, bf16[128,1024]{1,0:T(8,128)(2,1)S(1)}, u32[]{:S(2)}, u32[]{:S(2)}) collective-permute-start(bf16[128,1024]{1,0:T(8,128)(2,1)} %get-tuple-element.192), channel_id=1, source_target_pairs={{0,8},{4,12},{8,0},{12,4},{1,9},{5,13},{9,1},{13,5},{2,10},{6,14},... | collective-permute-start | bytes 786440 | tf_op jit(solution)/shard_map/ppermute | solution.py:348
  420.2 18.0 %collective-permute-start.56 = (bf16[1024,256]{1,0:T(8,128)(2,1)S(1)}, bf16[1024,256]{1,0:T(8,128)(2,1)S(1)}, u32[]{:S(2)}, u32[]{:S(2)}) collective-permute-start(bf16[1024,256]{1,0:T(8,128)(2,1)S(1)} %get-tuple-element.180.refs_0_), channel_id=1, source_target_pairs={{0,16},{16,0},{1,17},{17,1},{2,18},{18,2},{3,19},{19,3},{4,20},{20... | collective-permute-start | bytes 1572872 | tf_op jit(solution)/shard_map/ppermute | solution.py:348
  420.2 30.7 %collective-permute-start.45 = (bf16[256,1024]{1,0:T(8,128)(2,1)}, bf16[256,1024]{1,0:T(8,128)(2,1)}, u32[]{:S(2)}, u32[]{:S(2)}) collective-permute-start(bf16[256,1024]{1,0:T(8,128)(2,1)} %get-tuple-element.173), channel_id=1, source_target_pairs={{0,2},{1,3},{2,0},{3,1},{4,6},{5,7},{6,4},{7,5},{8,10},{9,11},{10,... | collective-permute-start | bytes 1572872 | tf_op jit(solution)/shard_map/ppermute | solution.py:348
  431.6 19.3 %collective-permute-start.46 = (bf16[256,1024]{1,0:T(8,128)(2,1)}, bf16[256,1024]{1,0:T(8,128)(2,1)}, u32[]{:S(2)}, u32[]{:S(2)}) collective-permute-start(bf16[256,1024]{1,0:T(8,128)(2,1)} %get-tuple-element.174), channel_id=1, source_target_pairs={{0,2},{1,3},{2,0},{3,1},{4,6},{5,7},{6,4},{7,5},{8,10},{9,11},{10,... | collective-permute-start | bytes 1572872 | tf_op jit(solution)/shard_map/ppermute | solution.py:348
  435.6 14.3 %collective-permute-start.55 = (bf16[128,1152]{1,0:T(8,128)(2,1)S(1)}, bf16[128,1152]{1,0:T(8,128)(2,1)S(1)}, u32[]{:S(2)}, u32[]{:S(2)}) collective-permute-start(bf16[128,1152]{1,0:T(8,128)(2,1)S(1)} %join.6.value_ref.refs_0_), channel_id=1, source_target_pairs={{0,4},{4,0},{8,12},{12,8},{1,5},{5,1},{9,13},{13,9},{2,6},{6,2},{1... | collective-permute-start | bytes 884744 | tf_op jit(solution)/shard_map/ppermute | solution.py:348
  435.6 14.1 %collective-permute-start.61 = (bf16[128,1024]{1,0:T(8,128)(2,1)S(1)}, bf16[128,1024]{1,0:T(8,128)(2,1)S(1)}, u32[]{:S(2)}, u32[]{:S(2)}) collective-permute-start(bf16[128,1024]{1,0:T(8,128)(2,1)S(1)} %fold.11.value_ref), channel_id=1, source_target_pairs={{0,8},{4,12},{8,0},{12,4},{1,9},{5,13},{9,1},{13,5},{2,10},{6,14},... | collective-permute-start | bytes 786440 | tf_op jit(solution)/shard_map/ppermute | solution.py:348
  449.8 10.7 %collective-permute-start.62 = (bf16[256,1024]{1,0:T(8,128)(2,1)S(1)}, bf16[256,1024]{1,0:T(8,128)(2,1)S(1)}, u32[]{:S(2)}, u32[]{:S(2)}) collective-permute-start(bf16[256,1024]{1,0:T(8,128)(2,1)S(1)} %join.9.value_ref), channel_id=1, source_target_pairs={{0,4},{4,0},{8,12},{12,8},{1,5},{5,1},{9,13},{13,9},{2,6},{6,2},{1... | collective-permute-start | bytes 1572872 | tf_op jit(solution)/shard_map/ppermute | solution.py:348
  450.8 16.6 %collective-permute-start.58 = (bf16[256,1152]{1,0:T(8,128)(2,1)}, bf16[256,1152]{1,0:T(8,128)(2,1)}, u32[]{:S(2)}, u32[]{:S(2)}) collective-permute-start(bf16[256,1152]{1,0:T(8,128)(2,1)} %join.7.refs_2_.value_ref.refs_0_), channel_id=1, source_target_pairs={{0,16},{16,0},{1,17},{17,1},{2,18},{18,2},{3,19},{19,3},{4,20},{20... | collective-permute-start | bytes 1769480 | tf_op jit(solution)/shard_map/ppermute | solution.py:348
  461.5 25.1 %collective-permute-start.63 = (bf16[512,1024]{1,0:T(8,128)(2,1)}, bf16[512,1024]{1,0:T(8,128)(2,1)}, u32[]{:S(2)}, u32[]{:S(2)}) collective-permute-start(bf16[512,1024]{1,0:T(8,128)(2,1)} %join.10.value_ref), channel_id=1, source_target_pairs={{0,16},{16,0},{1,17},{17,1},{2,18},{18,2},{3,19},{19,3},{4,20},{20... | collective-permute-start | bytes 3145736 | tf_op jit(solution)/shard_map/ppermute | solution.py:348
  (138 other events, 873.6 us)
Sparse Core Ops, SparseCore 0:
  213.2 92.0 reduce-scatter.1
  314.7 80.5 all-gather.1

commit v2 on v1

--- a/solution.py
+++ b/solution.py
@@ -167,7 +167,7 @@
     rows = pieces[0].shape[1]
     heads = pieces[0].shape[2] // (3 * HEAD_DIM)
     width = heads * HEAD_DIM
-    bk = 256
+    bk = 512
     smem = pl.BlockSpec(memory_space=pltpu.SMEM)
     vmem = pl.BlockSpec(memory_space=pltpu.VMEM)
     hbm = pl.BlockSpec(memory_space=pl.ANY)
@@ -312,7 +312,7 @@
     rows = pieces[0].shape[1]
     heads = pieces[0].shape[2] // (3 * HEAD_DIM)
     width = heads * HEAD_DIM
-    bk = 256
+    bk = 512
     smem = pl.BlockSpec(memory_space=pltpu.SMEM)
     vmem = pl.BlockSpec(memory_space=pltpu.VMEM)
     hbm = pl.BlockSpec(memory_space=pl.ANY)

time: 504 us -> 490 us (0.972)
  Pallas kernels: 186 us -> 168 us
    pallas_call x4, Pallas kernels: 16.8 us -> 8.52 us  [norm_rows(): pl.pallas_call(norm_kernel, grid=(rows // tile,), out_shape=(jax.ShapeDty...]
    pallas_call x2, Pallas kernels: 49.1 us -> 42 us  [attend_back(): pl.pallas_call(functools.partial(bwd_kernel, heads, bk, chunk), out_shape...]
  transfers between devices with their start and end apart: 66 -> 66, of which waited for: 34 -> 34; matrix products, arithmetic and copies ran while one was open for 9% -> 9% of each run, Pallas kernels for 30% -> 29%
where the time goes in v2:
time: 490 us; the launch traced here: 481 us
  Pallas kernels  168 us (34%)
  waiting for transfers between devices  165 us (34%)
  local copies, waits for them, and re-layouts  43.3 us (9%)
  starting transfers between devices  42.8 us (9%)
  matrix products  27.2 us (6%)
  other arithmetic  18.3 us (4%)
  between operations  15.7 us (3%)
    ppermute x64, waiting for transfers between devices, swap(): return lax.ppermute(value, axis, pairs)  165 us
    ppermute x64, starting transfers between devices, swap(): return lax.ppermute(value, axis, pairs)  42.7 us
    pallas_call x2, Pallas kernels, attend_back(): pl.pallas_call(functools.partial(bwd_kernel, heads, bk, chunk), out_shape...  42 us
    pallas_call x2, Pallas kernels, feed(): pl.pallas_call(functools.partial(feed_kernel, chunk), out_shape=(jax.Shap...  38.2 us
    unnamed x210, local copies, waits for them, and re-layouts  35.6 us
    pallas_call x2, Pallas kernels, attend(): pl.pallas_call(functools.partial(fwd_kernel, heads, bk, chunk), out_shape...  29 us
    dot_general x4, matrix products, shards(): jnp.dot(activated[chunk][side], w_down, preferred_element_type=F32)  12.1 us
    pallas_call x4, Pallas kernels, norm_back_rows(): pl.pallas_call(back_kernel, grid=(rows // tile,), out_shape=(jax.ShapeDty...  11.1 us
  transfers between devices with their start and end apart: 66, of which 34 were waited for; matrix products, arithmetic and copies ran while one was open for 9% of the time, Pallas kernels for 29%

profile of v2, /device:TPU:0, one launch (start us, length us, event | category | flops | bytes accessed | tf_op | source)
XLA Modules:
  0.0 480.5 jit_solution(12262756730100683073)
XLA Ops:
  12.5 11.8 %collective-permute-done.enc_ref = bf16[1024,256]{1,0:T(8,128)(2,1)S(1)} collective-permute-done((bf16[1024,256]{1,0:T(8,128)(2,1)S(1)}, bf16[1024,256]{1,0:T(8,128)(2,1)S(1)}, u32[]{:S(2)}, u32[]{:S(2)}) %collective-permute-start) | collective-permute-done | bytes 524320 | tf_op jit(solution)/shard_map/ppermute | solution.py:348
  24.3 3.3 skip.2
  32.6 10.1 %collective-permute-done.6.refs_0_ = bf16[1024,256]{1,0:T(8,128)(2,1)} collective-permute-done((bf16[1024,256]{1,0:T(8,128)(2,1)S(1)}, bf16[1024,256]{1,0:T(8,128)(2,1)}, u32[]{:S(2)}, u32[]{:S(2)}) %collective-permute-start.6) | collective-permute-done | bytes 524320 | tf_op jit(solution)/shard_map/ppermute | solution.py:348
  42.7 4.1 skip.3
  56.2 3.9 norm_rows.4
  72.7 14.3 %collective-permute-done.12.other_ref = bf16[512,1024]{1,0:T(8,128)(2,1)S(1)} collective-permute-done((bf16[512,1024]{1,0:T(8,128)(2,1)S(1)}, bf16[512,1024]{1,0:T(8,128)(2,1)S(1)}, u32[]{:S(2)}, u32[]{:S(2)}) %collective-permute-start.12) | collective-permute-done | bytes 1048608 | tf_op jit(solution)/shard_map/ppermute | solution.py:348
  94.7 13.2 %attend.2 = (bf16[2,512,256]{2,1,0:T(8,128)(2,1)S(1)}, f32[4,4,256]{2,1,0:T(4,128)S(1)}, bf16[512,1024]{1,0:T(8,128)(2,1)S(1)}, bf16[128,1024]{1,0:T(8,128)(2,1)...) custom-call(s32[2]{0:T(128)S(1)} %pad_add_fusion.core_ref.refs_0_, ...), custom_call_target="tpu_custom_call" | custom-call | tf_op jit(solution)/shard_map/attend/pallas_call | solution.py:174
  113.1 15.8 %attend.3 = (bf16[2,512,256]{2,1,0:T(8,128)(2,1)S(1)}, f32[4,4,256]{2,1,0:T(4,128)S(1)}, bf16[512,1024]{1,0:T(8,128)(2,1)S(1)}, bf16[128,1024]{1,0:T(8,128)(2,1)...) custom-call(s32[2]{0:T(128)S(1)} %pad_add_fusion.core_ref.refs_0_, ...), custom_call_target="tpu_custom_call" | custom-call | tf_op jit(solution)/shard_map/attend/pallas_call | solution.py:174
  132.8 4.1 collective-permute-done.18.other_ref
  140.8 18.5 %feed.2 = (bf16[2,512,1024]{2,1,0:T(8,128)(2,1)S(1)}, f32[2048,1024]{1,0:T(8,128)}, f32[8,1024]{1,0:T(8,128)S(1)}, bf16[512,1024]{1,0:T(8,128)(2,1)S(1)}, bf16[1...) custom-call(s32[2]{0:T(128)S(1)} %pad_add_fusion.core_ref.refs_0_, ...), custom_call_target="tpu_custom_call" | custom-call | tf_op jit(solution)/shard_map/feed/pallas_call | solution.py:659
  175.3 19.6 %feed.3 = (bf16[2,512,1024]{2,1,0:T(8,128)(2,1)S(1)}, bf16[2048,1024]{1,0:T(8,128)(2,1)}, f32[8,1024]{1,0:T(8,128)S(1)}, bf16[512,1024]{1,0:T(8,128)(2,1)S(1)}, ...) custom-call(s32[2]{0:T(128)S(1)} %pad_add_fusion.core_ref.refs_0_, ...), custom_call_target="tpu_custom_call" | custom-call | tf_op jit(solution)/shard_map/feed/pallas_call | solution.py:659
  215.5 18.5 %attend_back.2 = (bf16[2,512,256]{2,1,0:T(8,128)(2,1)S(1)}, f32[2048,512]{1,0:T(8,128)S(1)}) custom-call(s32[2]{0:T(128)S(1)} %pad_add_fusion.core_ref.refs_0_, f32[4]{0:T(128)S(1)} %multiply_exponential_fusion.slope_ref.refs_1_, s32[1,2048]{1,0:T(1,128)S(1)} %copy-done.75, bf16[2,256,768]{2,1,0:T(8,128)(2,1)S(1)} %bitcast.130, ...), custom_call_target="tpu_custom_call" | custom-call | tf_op jit(solution)/shard_map/attend_back/pallas_call | solution.py:328
  234.0 3.9 collective-permute-done.35.other_ref
  243.5 23.5 %attend_back.3.refs_4_ = bf16[4,512,768]{2,1,0:T(8,128)(2,1)S(1)} custom-call(s32[2]{0:T(128)S(1)} %pad_add_fusion.core_ref.refs_0_, f32[4]{0:T(128)S(1)} %multiply_exponential_fusion.slope_ref.refs_1_, s32[1,2048]{1,0:T(1,128)S(1)} %copy-done.75, bf16[2,256,768]{2,1,0:T(8,128)(2,1)S(1)} %bitcast.131, bf16[2,256,768]{2,1,0:T(8,128)(2,1)S(1)} %bitcast.135, ...), custom_call_target="tpu_custom_call" | custom-call | tf_op jit(solution)/shard_map/attend_back/pallas_call | solution.py:328
  274.6 7.3 %late_grads.1 = (bf16[512,1024]{1,0:T(8,128)(2,1)S(1)}, bf16[512,1024]{1,0:T(8,128)(2,1)S(1)}) custom-call(s32[1]{0:T(128)} %bitcast.2.mine_ref, bf16[512,1024]{1,0:T(8,128)(2,1)} %get-tuple-element.115.refs_0_, bf16[512,1024]{1,0:T(8,128)(2,1)} %collective-permute-done.11.refs_1_, bf16[512,1024]{1,0:T(8,128)(2,1)} %get-tuple-element.116.refs_2_, ...), custom_call_target="tpu_custom_call" | custom-call | tf_op jit(solution)/shard_map/late_grads/pallas_call | solution.py:504
  282.9 14.2 %collective-permute-done.43.other_ref = bf16[512,1024]{1,0:T(8,128)(2,1)S(1)} collective-permute-done((bf16[512,1024]{1,0:T(8,128)(2,1)S(1)}, bf16[512,1024]{1,0:T(8,128)(2,1)S(1)}, u32[]{:S(2)}, u32[]{:S(2)}) %collective-permute-start.43) | collective-permute-done | bytes 1048608 | tf_op jit(solution)/shard_map/ppermute | solution.py:348
  302.9 3.6 convolution_convert_fusion.2
  311.0 3.6 add_convert_fusion
  318.5 21.3 %collective-permute-done.44.came_ref = bf16[512,1024]{1,0:T(8,128)(2,1)S(1)} collective-permute-done((bf16[512,1024]{1,0:T(8,128)(2,1)}, bf16[512,1024]{1,0:T(8,128)(2,1)S(1)}, u32[]{:S(2)}, u32[]{:S(2)}) %collective-permute-start.44) | collective-permute-done | bytes 1048608 | tf_op jit(solution)/shard_map/ppermute | solution.py:348
  352.7 4.0 skip_grad.2.refs_0_
  356.7 4.7 skip_grad.3
  361.9 3.5 skip_back.2
  365.4 3.5 skip_back.3
  369.0 7.1 %collective-permute-done.51.came_ref = bf16[256,1152]{1,0:T(8,128)(2,1)S(1)} collective-permute-done((bf16[256,1152]{1,0:T(8,128)(2,1)S(1)}, bf16[256,1152]{1,0:T(8,128)(2,1)S(1)}, u32[]{:S(2)}, u32[]{:S(2)}) %collective-permute-start.51) | collective-permute-done | bytes 589856 | tf_op jit(solution)/shard_map/ppermute | solution.py:348
  378.5 9.5 %collective-permute-done.52.came_ref = bf16[128,1152]{1,0:T(8,128)(2,1)S(1)} collective-permute-done((bf16[128,1152]{1,0:T(8,128)(2,1)S(1)}, bf16[128,1152]{1,0:T(8,128)(2,1)S(1)}, u32[]{:S(2)}, u32[]{:S(2)}) %collective-permute-start.52) | collective-permute-done | bytes 294944 | tf_op jit(solution)/shard_map/ppermute | solution.py:348
  390.4 6.8 %collective-permute-done.53.came_ref = bf16[64,1152]{1,0:T(8,128)(2,1)S(1)} collective-permute-done((bf16[64,1152]{1,0:T(8,128)(2,1)S(1)}, bf16[64,1152]{1,0:T(8,128)(2,1)S(1)}, u32[]{:S(2)}, u32[]{:S(2)}) %collective-permute-start.53) | collective-permute-done | bytes 147488 | tf_op jit(solution)/shard_map/ppermute | solution.py:348
  397.2 3.5 collective-permute-start.54
  404.5 8.7 %collective-permute-done.54.came_ref = bf16[64,1152]{1,0:T(8,128)(2,1)S(1)} collective-permute-done((bf16[64,1152]{1,0:T(8,128)(2,1)S(1)}, bf16[64,1152]{1,0:T(8,128)(2,1)S(1)}, u32[]{:S(2)}, u32[]{:S(2)}) %collective-permute-start.54) | collective-permute-done | bytes 147488 | tf_op jit(solution)/shard_map/ppermute | solution.py:348
  421.3 10.5 %collective-permute-done.61.came_ref = bf16[128,1024]{1,0:T(8,128)(2,1)S(1)} collective-permute-done((bf16[128,1024]{1,0:T(8,128)(2,1)S(1)}, bf16[128,1024]{1,0:T(8,128)(2,1)S(1)}, u32[]{:S(2)}, u32[]{:S(2)}) %collective-permute-start.61) | collective-permute-done | bytes 262176 | tf_op jit(solution)/shard_map/ppermute | solution.py:348
  436.7 6.0 %collective-permute-done.62.came_ref = bf16[256,1024]{1,0:T(8,128)(2,1)S(1)} collective-permute-done((bf16[256,1024]{1,0:T(8,128)(2,1)S(1)}, bf16[256,1024]{1,0:T(8,128)(2,1)S(1)}, u32[]{:S(2)}, u32[]{:S(2)}) %collective-permute-start.62) | collective-permute-done | bytes 524320 | tf_op jit(solution)/shard_map/ppermute | solution.py:348
  444.3 4.7 collective-permute-done.58.came_ref
  455.9 12.4 %collective-permute-done.63.came_ref = bf16[512,1024]{1,0:T(8,128)(2,1)} collective-permute-done((bf16[512,1024]{1,0:T(8,128)(2,1)}, bf16[512,1024]{1,0:T(8,128)(2,1)}, u32[]{:S(2)}, u32[]{:S(2)}) %collective-permute-start.63) | collective-permute-done | bytes 1048608 | tf_op jit(solution)/shard_map/ppermute | solution.py:348
  (401 shorter events, 165.4 us)
Async XLA Ops:
  7.2 294.1 %reduce-scatter.2.cloned.1.call-start = ((), (), s32[]{:S(2)}) async-start(), calls=%async_computation.1 | async-start | bytes 4718592 | tf_op jit(solution)/shard_map/reduce_scatter | solution.py:962
  9.5 14.9 %collective-permute-start = (bf16[1024,256]{1,0:T(8,128)(2,1)S(1)}, bf16[1024,256]{1,0:T(8,128)(2,1)S(1)}, u32[]{:S(2)}, u32[]{:S(2)}) collective-permute-start(bf16[1024,256]{1,0:T(8,128)(2,1)S(1)} %bitcast.183), channel_id=1, source_target_pairs={{0,16},{16,0},{1,17},{17,1},{2,18},{18,2},{3,19},{19,3},{4,20},{20... | collective-permute-start | bytes 1572872 | tf_op jit(solution)/shard_map/ppermute | solution.py:348
  28.7 14.0 %collective-permute-start.6 = (bf16[1024,256]{1,0:T(8,128)(2,1)S(1)}, bf16[1024,256]{1,0:T(8,128)(2,1)}, u32[]{:S(2)}, u32[]{:S(2)}) collective-permute-start(bf16[1024,256]{1,0:T(8,128)(2,1)S(1)} %bitcast.182), channel_id=1, source_target_pairs={{0,16},{16,0},{1,17},{17,1},{2,18},{18,2},{3,19},{19,3},{4,20},{20... | collective-permute-start | bytes 1572872 | tf_op jit(solution)/shard_map/ppermute | solution.py:348
  30.9 25.3 %collective-permute-start.5 = (bf16[512,1024]{1,0:T(8,128)(2,1)S(1)}, bf16[512,1024]{1,0:T(8,128)(2,1)}, u32[]{:S(2)}, u32[]{:S(2)}) collective-permute-start(bf16[512,1024]{1,0:T(8,128)(2,1)S(1)} %add_convert_fusion.9.refs_1_.mine_ref), channel_id=1, source_target_pairs={{0,2},{1,3},{2,0},{3,1},{4,6},{5,7},{6,4},{7,5},{8,10},{9,11},{10,... | collective-permute-start | bytes 3145736 | tf_op jit(solution)/shard_map/ppermute | solution.py:348
  61.4 8.9 %collective-permute-start.11 = (bf16[512,1024]{1,0:T(8,128)(2,1)}, bf16[512,1024]{1,0:T(8,128)(2,1)}, u32[]{:S(2)}, u32[]{:S(2)}) collective-permute-start(bf16[512,1024]{1,0:T(8,128)(2,1)} %get-tuple-element.115.refs_0_), channel_id=1, source_target_pairs={{0,1},{1,0},{2,3},{3,2},{4,5},{5,4},{6,7},{7,6},{8,9},{9,8},{10,11... | collective-permute-start | bytes 3145736 | tf_op jit(solution)/shard_map/ppermute | solution.py:348
  61.4 25.6 %collective-permute-start.12 = (bf16[512,1024]{1,0:T(8,128)(2,1)S(1)}, bf16[512,1024]{1,0:T(8,128)(2,1)S(1)}, u32[]{:S(2)}, u32[]{:S(2)}) collective-permute-start(bf16[512,1024]{1,0:T(8,128)(2,1)S(1)} %add_convert_fusion.8.refs_2_.mine_ref), channel_id=1, source_target_pairs={{0,2},{1,3},{2,0},{3,1},{4,6},{5,7},{6,4},{7,5},{8,10},{9,11},{10,... | collective-permute-start | bytes 3145736 | tf_op jit(solution)/shard_map/ppermute | solution.py:348
  111.3 25.5 %collective-permute-start.18 = (bf16[512,1024]{1,0:T(8,128)(2,1)S(1)}, bf16[512,1024]{1,0:T(8,128)(2,1)S(1)}, u32[]{:S(2)}, u32[]{:S(2)}) collective-permute-start(bf16[512,1024]{1,0:T(8,128)(2,1)S(1)} %add_convert_fusion.7.refs_0_.mine_ref), channel_id=1, source_target_pairs={{0,2},{1,3},{2,0},{3,1},{4,6},{5,7},{6,4},{7,5},{8,10},{9,11},{10,... | collective-permute-start | bytes 3145736 | tf_op jit(solution)/shard_map/ppermute | solution.py:348
  138.1 25.6 %collective-permute-start.24 = (bf16[512,1024]{1,0:T(8,128)(2,1)S(1)}, bf16[512,1024]{1,0:T(8,128)(2,1)S(1)}, u32[]{:S(2)}, u32[]{:S(2)}) collective-permute-start(bf16[512,1024]{1,0:T(8,128)(2,1)S(1)} %add_convert_fusion.6.refs_1_.mine_ref), channel_id=1, source_target_pairs={{0,2},{1,3},{2,0},{3,1},{4,6},{5,7},{6,4},{7,5},{8,10},{9,11},{10,... | collective-permute-start | bytes 3145736 | tf_op jit(solution)/shard_map/ppermute | solution.py:348
  172.6 25.6 %collective-permute-start.34 = (bf16[512,1024]{1,0:T(8,128)(2,1)S(1)}, bf16[512,1024]{1,0:T(8,128)(2,1)S(1)}, u32[]{:S(2)}, u32[]{:S(2)}) collective-permute-start(bf16[512,1024]{1,0:T(8,128)(2,1)S(1)} %add_convert_fusion.5.refs_0_.mine_ref), channel_id=1, source_target_pairs={{0,2},{1,3},{2,0},{3,1},{4,6},{5,7},{6,4},{7,5},{8,10},{9,11},{10,... | collective-permute-start | bytes 3145736 | tf_op jit(solution)/shard_map/ppermute | solution.py:348
  203.3 249.4 %all-gather.2.cloned.1.call-start = ((), (), s32[]{:S(2)}) async-start(), calls=%async_computation.2 | async-start | bytes 4718592 | tf_op jit(solution)/shard_map/all_gather | solution.py:1023
  212.4 25.6 %collective-permute-start.35 = (bf16[512,1024]{1,0:T(8,128)(2,1)S(1)}, bf16[512,1024]{1,0:T(8,128)(2,1)S(1)}, u32[]{:S(2)}, u32[]{:S(2)}) collective-permute-start(bf16[512,1024]{1,0:T(8,128)(2,1)S(1)} %copy-done.4), channel_id=1, source_target_pairs={{0,2},{1,3},{2,0},{3,1},{4,6},{5,7},{6,4},{7,5},{8,10},{9,11},{10,... | collective-permute-start | bytes 3145736 | tf_op jit(solution)/shard_map/ppermute | solution.py:348
  271.8 25.3 %collective-permute-start.43 = (bf16[512,1024]{1,0:T(8,128)(2,1)S(1)}, bf16[512,1024]{1,0:T(8,128)(2,1)S(1)}, u32[]{:S(2)}, u32[]{:S(2)}) collective-permute-start(bf16[512,1024]{1,0:T(8,128)(2,1)S(1)} %add_convert_fusion.3.refs_11_.mine_ref), channel_id=1, source_target_pairs={{0,2},{1,3},{2,0},{3,1},{4,6},{5,7},{6,4},{7,5},{8,10},{9,11},{10,... | collective-permute-start | bytes 3145736 | tf_op jit(solution)/shard_map/ppermute | solution.py:348
  308.7 6.9 %collective-permute-start.40 = (bf16[512,1024]{1,0:T(8,128)(2,1)}, bf16[512,1024]{1,0:T(8,128)(2,1)}, u32[]{:S(2)}, u32[]{:S(2)}) collective-permute-start(bf16[512,1024]{1,0:T(8,128)(2,1)} %convolution_convert_fusion.3), channel_id=1, source_target_pairs={{0,1},{1,0},{2,3},{3,2},{4,5},{5,4},{6,7},{7,6},{8,9},{9,8},{10,11... | collective-permute-start | bytes 3145736 | tf_op jit(solution)/shard_map/ppermute | solution.py:348
  309.2 32.0 %collective-permute-start.42 = (bf16[512,1024]{1,0:T(8,128)(2,1)S(1)}, bf16[512,1024]{1,0:T(8,128)(2,1)S(1)}, u32[]{:S(2)}, u32[]{:S(2)}) collective-permute-start(bf16[512,1024]{1,0:T(8,128)(2,1)S(1)} %add_convert_fusion.2.refs_12_.mine_ref), channel_id=1, source_target_pairs={{0,2},{1,3},{2,0},{3,1},{4,6},{5,7},{6,4},{7,5},{8,10},{9,11},{10,... | collective-permute-start | bytes 3145736 | tf_op jit(solution)/shard_map/ppermute | solution.py:348
  310.9 28.9 %collective-permute-start.44 = (bf16[512,1024]{1,0:T(8,128)(2,1)}, bf16[512,1024]{1,0:T(8,128)(2,1)S(1)}, u32[]{:S(2)}, u32[]{:S(2)}) collective-permute-start(bf16[512,1024]{1,0:T(8,128)(2,1)} %copy-done.84), channel_id=1, source_target_pairs={{0,16},{16,0},{1,17},{17,1},{2,18},{18,2},{3,19},{19,3},{4,20},{20... | collective-permute-start | bytes 3145736 | tf_op jit(solution)/shard_map/ppermute | solution.py:348
  310.9 40.7 %collective-permute-start.48 = (bf16[512,1024]{1,0:T(8,128)(2,1)S(1)}, bf16[512,1024]{1,0:T(8,128)(2,1)}, u32[]{:S(2)}, u32[]{:S(2)}) collective-permute-start(bf16[512,1024]{1,0:T(8,128)(2,1)S(1)} %copy-done.6), channel_id=1, source_target_pairs={{0,1},{1,0},{2,3},{3,2},{4,5},{5,4},{6,7},{7,6},{8,9},{9,8},{10,11... | collective-permute-start | bytes 3145736 | tf_op jit(solution)/shard_map/ppermute | solution.py:348
  344.9 11.8 %collective-permute-start.47 = (bf16[512,1024]{1,0:T(8,128)(2,1)S(1)}, bf16[512,1024]{1,0:T(8,128)(2,1)}, u32[]{:S(2)}, u32[]{:S(2)}) collective-permute-start(bf16[512,1024]{1,0:T(8,128)(2,1)S(1)} %get-tuple-element.172.refs_2_.own_ref), channel_id=1, source_target_pairs={{0,1},{1,0},{2,3},{3,2},{4,5},{5,4},{6,7},{7,6},{8,9},{9,8},{10,11... | collective-permute-start | bytes 3145736 | tf_op jit(solution)/shard_map/ppermute | solution.py:348
  361.5 14.6 %collective-permute-start.51 = (bf16[256,1152]{1,0:T(8,128)(2,1)S(1)}, bf16[256,1152]{1,0:T(8,128)(2,1)S(1)}, u32[]{:S(2)}, u32[]{:S(2)}) collective-permute-start(bf16[256,1152]{1,0:T(8,128)(2,1)S(1)} %get-tuple-element.179), channel_id=1, source_target_pairs={{0,16},{16,0},{1,17},{17,1},{2,18},{18,2},{3,19},{19,3},{4,20},{20... | collective-permute-start | bytes 1769480 | tf_op jit(solution)/shard_map/ppermute | solution.py:348
  376.4 11.6 %collective-permute-start.52 = (bf16[128,1152]{1,0:T(8,128)(2,1)S(1)}, bf16[128,1152]{1,0:T(8,128)(2,1)S(1)}, u32[]{:S(2)}, u32[]{:S(2)}) collective-permute-start(bf16[128,1152]{1,0:T(8,128)(2,1)S(1)} %get-tuple-element.184), channel_id=1, source_target_pairs={{0,4},{4,0},{8,12},{12,8},{1,5},{5,1},{9,13},{13,9},{2,6},{6,2},{1... | collective-permute-start | bytes 884744 | tf_op jit(solution)/shard_map/ppermute | solution.py:348
  377.9 22.7 %collective-permute-start.59 = (bf16[256,1024]{1,0:T(8,128)(2,1)S(1)}, bf16[256,1024]{1,0:T(8,128)(2,1)S(1)}, u32[]{:S(2)}, u32[]{:S(2)}) collective-permute-start(bf16[256,1024]{1,0:T(8,128)(2,1)S(1)} %copy-done.86), channel_id=1, source_target_pairs={{0,4},{4,0},{8,12},{12,8},{1,5},{5,1},{9,13},{13,9},{2,6},{6,2},{1... | collective-permute-start | bytes 1572872 | tf_op jit(solution)/shard_map/ppermute | solution.py:348
  388.3 8.8 %collective-permute-start.53 = (bf16[64,1152]{1,0:T(8,128)(2,1)S(1)}, bf16[64,1152]{1,0:T(8,128)(2,1)S(1)}, u32[]{:S(2)}, u32[]{:S(2)}) collective-permute-start(bf16[64,1152]{1,0:T(8,128)(2,1)S(1)} %get-tuple-element.186), channel_id=1, source_target_pairs={{0,8},{4,12},{8,0},{12,4},{1,9},{5,13},{9,1},{13,5},{2,10},{6,14},... | collective-permute-start | bytes 442376 | tf_op jit(solution)/shard_map/ppermute | solution.py:348
  389.2 28.5 %collective-permute-start.57 = (bf16[1024,256]{1,0:T(8,128)(2,1)}, bf16[1024,256]{1,0:T(8,128)(2,1)S(1)}, u32[]{:S(2)}, u32[]{:S(2)}) collective-permute-start(bf16[1024,256]{1,0:T(8,128)(2,1)} %copy-done.70), channel_id=1, source_target_pairs={{0,16},{16,0},{1,17},{17,1},{2,18},{18,2},{3,19},{19,3},{4,20},{20... | collective-permute-start | bytes 1572872 | tf_op jit(solution)/shard_map/ppermute | solution.py:348
  397.2 15.9 %collective-permute-start.54 = (bf16[64,1152]{1,0:T(8,128)(2,1)S(1)}, bf16[64,1152]{1,0:T(8,128)(2,1)S(1)}, u32[]{:S(2)}, u32[]{:S(2)}) collective-permute-start(bf16[64,1152]{1,0:T(8,128)(2,1)S(1)} %fold.9.value_ref.refs_0_), channel_id=1, source_target_pairs={{0,8},{4,12},{8,0},{12,4},{1,9},{5,13},{9,1},{13,5},{2,10},{6,14},... | collective-permute-start | bytes 442376 | tf_op jit(solution)/shard_map/ppermute | solution.py:348
  402.3 15.3 %collective-permute-start.60 = (bf16[128,1024]{1,0:T(8,128)(2,1)}, bf16[128,1024]{1,0:T(8,128)(2,1)S(1)}, u32[]{:S(2)}, u32[]{:S(2)}) collective-permute-start(bf16[128,1024]{1,0:T(8,128)(2,1)} %get-tuple-element.192), channel_id=1, source_target_pairs={{0,8},{4,12},{8,0},{12,4},{1,9},{5,13},{9,1},{13,5},{2,10},{6,14},... | collective-permute-start | bytes 786440 | tf_op jit(solution)/shard_map/ppermute | solution.py:348
  402.4 17.3 %collective-permute-start.56 = (bf16[1024,256]{1,0:T(8,128)(2,1)S(1)}, bf16[1024,256]{1,0:T(8,128)(2,1)S(1)}, u32[]{:S(2)}, u32[]{:S(2)}) collective-permute-start(bf16[1024,256]{1,0:T(8,128)(2,1)S(1)} %get-tuple-element.180.refs_0_), channel_id=1, source_target_pairs={{0,16},{16,0},{1,17},{17,1},{2,18},{18,2},{3,19},{19,3},{4,20},{20... | collective-permute-start | bytes 1572872 | tf_op jit(solution)/shard_map/ppermute | solution.py:348
  403.1 30.3 %collective-permute-start.45 = (bf16[256,1024]{1,0:T(8,128)(2,1)}, bf16[256,1024]{1,0:T(8,128)(2,1)}, u32[]{:S(2)}, u32[]{:S(2)}) collective-permute-start(bf16[256,1024]{1,0:T(8,128)(2,1)} %get-tuple-element.173), channel_id=1, source_target_pairs={{0,2},{1,3},{2,0},{3,1},{4,6},{5,7},{6,4},{7,5},{8,10},{9,11},{10,... | collective-permute-start | bytes 1572872 | tf_op jit(solution)/shard_map/ppermute | solution.py:348
  413.8 19.6 %collective-permute-start.46 = (bf16[256,1024]{1,0:T(8,128)(2,1)}, bf16[256,1024]{1,0:T(8,128)(2,1)}, u32[]{:S(2)}, u32[]{:S(2)}) collective-permute-start(bf16[256,1024]{1,0:T(8,128)(2,1)} %get-tuple-element.174), channel_id=1, source_target_pairs={{0,2},{1,3},{2,0},{3,1},{4,6},{5,7},{6,4},{7,5},{8,10},{9,11},{10,... | collective-permute-start | bytes 1572872 | tf_op jit(solution)/shard_map/ppermute | solution.py:348
  417.7 14.2 %collective-permute-start.55 = (bf16[128,1152]{1,0:T(8,128)(2,1)S(1)}, bf16[128,1152]{1,0:T(8,128)(2,1)S(1)}, u32[]{:S(2)}, u32[]{:S(2)}) collective-permute-start(bf16[128,1152]{1,0:T(8,128)(2,1)S(1)} %join.6.value_ref.refs_0_), channel_id=1, source_target_pairs={{0,4},{4,0},{8,12},{12,8},{1,5},{5,1},{9,13},{13,9},{2,6},{6,2},{1... | collective-permute-start | bytes 884744 | tf_op jit(solution)/shard_map/ppermute | solution.py:348
  417.8 14.0 %collective-permute-start.61 = (bf16[128,1024]{1,0:T(8,128)(2,1)S(1)}, bf16[128,1024]{1,0:T(8,128)(2,1)S(1)}, u32[]{:S(2)}, u32[]{:S(2)}) collective-permute-start(bf16[128,1024]{1,0:T(8,128)(2,1)S(1)} %fold.11.value_ref), channel_id=1, source_target_pairs={{0,8},{4,12},{8,0},{12,4},{1,9},{5,13},{9,1},{13,5},{2,10},{6,14},... | collective-permute-start | bytes 786440 | tf_op jit(solution)/shard_map/ppermute | solution.py:348
  431.8 10.8 %collective-permute-start.62 = (bf16[256,1024]{1,0:T(8,128)(2,1)S(1)}, bf16[256,1024]{1,0:T(8,128)(2,1)S(1)}, u32[]{:S(2)}, u32[]{:S(2)}) collective-permute-start(bf16[256,1024]{1,0:T(8,128)(2,1)S(1)} %join.9.value_ref), channel_id=1, source_target_pairs={{0,4},{4,0},{8,12},{12,8},{1,5},{5,1},{9,13},{13,9},{2,6},{6,2},{1... | collective-permute-start | bytes 1572872 | tf_op jit(solution)/shard_map/ppermute | solution.py:348
  432.8 16.2 %collective-permute-start.58 = (bf16[256,1152]{1,0:T(8,128)(2,1)}, bf16[256,1152]{1,0:T(8,128)(2,1)}, u32[]{:S(2)}, u32[]{:S(2)}) collective-permute-start(bf16[256,1152]{1,0:T(8,128)(2,1)} %join.7.refs_2_.value_ref.refs_0_), channel_id=1, source_target_pairs={{0,16},{16,0},{1,17},{17,1},{2,18},{18,2},{3,19},{19,3},{4,20},{20... | collective-permute-start | bytes 1769480 | tf_op jit(solution)/shard_map/ppermute | solution.py:348
  443.7 24.7 %collective-permute-start.63 = (bf16[512,1024]{1,0:T(8,128)(2,1)}, bf16[512,1024]{1,0:T(8,128)(2,1)}, u32[]{:S(2)}, u32[]{:S(2)}) collective-permute-start(bf16[512,1024]{1,0:T(8,128)(2,1)} %join.10.value_ref), channel_id=1, source_target_pairs={{0,16},{16,0},{1,17},{17,1},{2,18},{18,2},{3,19},{19,3},{4,20},{20... | collective-permute-start | bytes 3145736 | tf_op jit(solution)/shard_map/ppermute | solution.py:348
  (138 other events, 842.2 us)
Sparse Core Ops, SparseCore 0:
  203.4 91.3 reduce-scatter.1
  301.4 76.1 all-gather.1

commit v3 on v2

--- a/solution.py
+++ b/solution.py
@@ -676,7 +676,7 @@
             pltpu.VMEM((8, units), F32),
             pltpu.SemaphoreType.DMA((4,)),
         ],
-        compiler_params=pltpu.CompilerParams(vmem_limit_bytes=44 << 20),
+        compiler_params=pltpu.CompilerParams(vmem_limit_bytes=36 << 20),
         name="feed",
     )(core, w_up, c_up[None], w_down, own, sib, cot, *before)
 

time: 490 us -> 492 us (level)
  Pallas kernels: 168 us -> 146 us
  waiting for transfers between devices: 165 us -> 182 us
  starting transfers between devices: 42.8 us -> 48.7 us
    ppermute x64, waiting for transfers between devices: 165 us -> 180 us  [swap(): return lax.ppermute(value, axis, pairs)]
    pallas_call x2, Pallas kernels: 42 us -> 31.1 us  [attend_back(): pl.pallas_call(functools.partial(bwd_kernel, heads, bk, chunk), out_shape...]
    pallas_call x2, Pallas kernels: 29 us -> 22.4 us  [attend(): pl.pallas_call(functools.partial(fwd_kernel, heads, bk, chunk), out_shape...]
    ppermute x64, starting transfers between devices: 42.7 us -> 48.6 us  [swap(): return lax.ppermute(value, axis, pairs)]
    unnamed x210 -> x214, local copies, waits for them, and re-layouts: 35.6 us -> 38 us
  transfers between devices with their start and end apart: 66 -> 66, of which waited for: 34 -> 35; matrix products, arithmetic and copies ran while one was open for 9% -> 9% of each run, Pallas kernels for 29% -> 25%
where the time goes in v3:
time: 492 us; the launch traced here: 483 us
  waiting for transfers between devices  182 us (37%)
  Pallas kernels  146 us (30%)
  starting transfers between devices  48.7 us (10%)
  local copies, waits for them, and re-layouts  45.6 us (9%)
  matrix products  26.5 us (5%)
  other arithmetic  18.4 us (4%)
  between operations  15.7 us (3%)
    ppermute x64, waiting for transfers between devices, swap(): return lax.ppermute(value, axis, pairs)  180 us
    ppermute x64, starting transfers between devices, swap(): return lax.ppermute(value, axis, pairs)  48.6 us
    unnamed x214, local copies, waits for them, and re-layouts  38 us
    pallas_call x2, Pallas kernels, feed(): pl.pallas_call(functools.partial(feed_kernel, chunk), out_shape=(jax.Shap...  33.5 us
    pallas_call x2, Pallas kernels, attend_back(): pl.pallas_call(functools.partial(bwd_kernel, heads, bk, chunk), out_shape...  31.1 us
    pallas_call x2, Pallas kernels, attend(): pl.pallas_call(functools.partial(fwd_kernel, heads, bk, chunk), out_shape...  22.4 us
    dot_general x4, matrix products, shards(): jnp.dot(activated[chunk][side], w_down, preferred_element_type=F32)  11.4 us
    pallas_call x4, Pallas kernels, norm_back_rows(): pl.pallas_call(back_kernel, grid=(rows // tile,), out_shape=(jax.ShapeDty...  11.1 us
  transfers between devices with their start and end apart: 66, of which 35 were waited for; matrix products, arithmetic and copies ran while one was open for 9% of the time, Pallas kernels for 25%

profile of v3, /device:TPU:0, one launch (start us, length us, event | category | flops | bytes accessed | tf_op | source)
XLA Modules:
  0.0 482.9 jit_solution(7544598676479196774)
XLA Ops:
  12.5 11.8 %collective-permute-done.enc_ref = bf16[1024,256]{1,0:T(8,128)(2,1)S(1)} collective-permute-done((bf16[1024,256]{1,0:T(8,128)(2,1)S(1)}, bf16[1024,256]{1,0:T(8,128)(2,1)S(1)}, u32[]{:S(2)}, u32[]{:S(2)}) %collective-permute-start) | collective-permute-done | bytes 524320 | tf_op jit(solution)/shard_map/ppermute | solution.py:348
  32.6 10.1 %collective-permute-done.6.refs_0_ = bf16[1024,256]{1,0:T(8,128)(2,1)} collective-permute-done((bf16[1024,256]{1,0:T(8,128)(2,1)S(1)}, bf16[1024,256]{1,0:T(8,128)(2,1)}, u32[]{:S(2)}, u32[]{:S(2)}) %collective-permute-start.6) | collective-permute-done | bytes 524320 | tf_op jit(solution)/shard_map/ppermute | solution.py:348
  42.7 4.1 skip.3
  56.2 3.9 norm_rows.4
  72.7 14.3 %collective-permute-done.12.other_ref = bf16[512,1024]{1,0:T(8,128)(2,1)S(1)} collective-permute-done((bf16[512,1024]{1,0:T(8,128)(2,1)S(1)}, bf16[512,1024]{1,0:T(8,128)(2,1)S(1)}, u32[]{:S(2)}, u32[]{:S(2)}) %collective-permute-start.12) | collective-permute-done | bytes 1048608 | tf_op jit(solution)/shard_map/ppermute | solution.py:348
  94.7 11.3 %attend.2 = (bf16[2,512,256]{2,1,0:T(8,128)(2,1)S(1)}, f32[4,4,256]{2,1,0:T(4,128)S(1)}, bf16[512,1024]{1,0:T(8,128)(2,1)S(1)}, bf16[128,1024]{1,0:T(8,128)(2,1)...) custom-call(s32[2]{0:T(128)S(1)} %pad_add_fusion.core_ref.refs_0_, ...), custom_call_target="tpu_custom_call" | custom-call | tf_op jit(solution)/shard_map/attend/pallas_call | solution.py:174
  111.2 11.0 %attend.3 = (bf16[2,512,256]{2,1,0:T(8,128)(2,1)S(1)}, f32[4,4,256]{2,1,0:T(4,128)S(1)}, bf16[512,1024]{1,0:T(8,128)(2,1)S(1)}, bf16[128,1024]{1,0:T(8,128)(2,1)...) custom-call(s32[2]{0:T(128)S(1)} %pad_add_fusion.core_ref.refs_0_, ...), custom_call_target="tpu_custom_call" | custom-call | tf_op jit(solution)/shard_map/attend/pallas_call | solution.py:174
  126.2 8.7 %collective-permute-done.18.other_ref = bf16[512,1024]{1,0:T(8,128)(2,1)S(1)} collective-permute-done((bf16[512,1024]{1,0:T(8,128)(2,1)S(1)}, bf16[512,1024]{1,0:T(8,128)(2,1)S(1)}, u32[]{:S(2)}, u32[]{:S(2)}) %collective-permute-start.18) | collective-permute-done | bytes 1048608 | tf_op jit(solution)/shard_map/ppermute | solution.py:348
  138.9 16.3 %feed.2 = (bf16[2,512,1024]{2,1,0:T(8,128)(2,1)S(1)}, f32[2048,1024]{1,0:T(8,128)}, f32[8,1024]{1,0:T(8,128)S(1)}, bf16[512,1024]{1,0:T(8,128)(2,1)S(1)}, bf16[1...) custom-call(s32[2]{0:T(128)S(1)} %pad_add_fusion.core_ref.refs_0_, ...), custom_call_target="tpu_custom_call" | custom-call | tf_op jit(solution)/shard_map/feed/pallas_call | solution.py:659
  157.6 4.2 collective-permute-done.24.refs_4_.other_ref
  173.4 17.2 %feed.3 = (bf16[2,512,1024]{2,1,0:T(8,128)(2,1)S(1)}, bf16[2048,1024]{1,0:T(8,128)(2,1)S(1)}, f32[8,1024]{1,0:T(8,128)S(1)}, bf16[512,1024]{1,0:T(8,128)(2,1)S(1...) custom-call(s32[2]{0:T(128)S(1)} %pad_add_fusion.core_ref.refs_0_, ...), custom_call_target="tpu_custom_call" | custom-call | tf_op jit(solution)/shard_map/feed/pallas_call | solution.py:659
  213.6 15.4 %attend_back.2 = (bf16[2,512,256]{2,1,0:T(8,128)(2,1)S(1)}, f32[2048,512]{1,0:T(8,128)S(1)}) custom-call(s32[2]{0:T(128)S(1)} %pad_add_fusion.core_ref.refs_0_, f32[4]{0:T(128)S(1)} %multiply_exponential_fusion.slope_ref.refs_1_, s32[1,2048]{1,0:T(1,128)S(1)} %copy-done.80, bf16[2,256,768]{2,1,0:T(8,128)(2,1)S(1)} %bitcast.131, ...), custom_call_target="tpu_custom_call" | custom-call | tf_op jit(solution)/shard_map/attend_back/pallas_call | solution.py:328
  229.0 7.0 %collective-permute-done.35.other_ref = bf16[512,1024]{1,0:T(8,128)(2,1)S(1)} collective-permute-done((bf16[512,1024]{1,0:T(8,128)(2,1)S(1)}, bf16[512,1024]{1,0:T(8,128)(2,1)S(1)}, u32[]{:S(2)}, u32[]{:S(2)}) %collective-permute-start.35) | collective-permute-done | bytes 1048608 | tf_op jit(solution)/shard_map/ppermute | solution.py:348
  241.6 15.7 %attend_back.3.refs_4_ = bf16[4,512,768]{2,1,0:T(8,128)(2,1)S(1)} custom-call(s32[2]{0:T(128)S(1)} %pad_add_fusion.core_ref.refs_0_, f32[4]{0:T(128)S(1)} %multiply_exponential_fusion.slope_ref.refs_1_, s32[1,2048]{1,0:T(1,128)S(1)} %copy-done.80, bf16[2,256,768]{2,1,0:T(8,128)(2,1)S(1)} %bitcast.132, bf16[2,256,768]{2,1,0:T(8,128)(2,1)S(1)} %bitcast.136, ...), custom_call_target="tpu_custom_call" | custom-call | tf_op jit(solution)/shard_map/attend_back/pallas_call | solution.py:328
  264.9 7.3 %late_grads.1 = (bf16[512,1024]{1,0:T(8,128)(2,1)S(1)}, bf16[512,1024]{1,0:T(8,128)(2,1)S(1)}) custom-call(s32[1]{0:T(128)} %bitcast.2.mine_ref, bf16[512,1024]{1,0:T(8,128)(2,1)} %get-tuple-element.115.refs_0_, bf16[512,1024]{1,0:T(8,128)(2,1)} %collective-permute-done.11.refs_1_, bf16[512,1024]{1,0:T(8,128)(2,1)} %get-tuple-element.116.refs_2_, ...), custom_call_target="tpu_custom_call" | custom-call | tf_op jit(solution)/shard_map/late_grads/pallas_call | solution.py:504
  273.2 14.2 %collective-permute-done.43.other_ref = bf16[512,1024]{1,0:T(8,128)(2,1)S(1)} collective-permute-done((bf16[512,1024]{1,0:T(8,128)(2,1)S(1)}, bf16[512,1024]{1,0:T(8,128)(2,1)S(1)}, u32[]{:S(2)}, u32[]{:S(2)}) %collective-permute-start.43) | collective-permute-done | bytes 1048608 | tf_op jit(solution)/shard_map/ppermute | solution.py:348
  295.4 3.6 convolution_convert_fusion.2
  311.4 22.4 %collective-permute-done.44.came_ref = bf16[512,1024]{1,0:T(8,128)(2,1)S(1)} collective-permute-done((bf16[512,1024]{1,0:T(8,128)(2,1)}, bf16[512,1024]{1,0:T(8,128)(2,1)S(1)}, u32[]{:S(2)}, u32[]{:S(2)}) %collective-permute-start.44) | collective-permute-done | bytes 1048608 | tf_op jit(solution)/shard_map/ppermute | solution.py:348
  342.3 3.3 collective-permute-done.50
  346.7 4.0 skip_grad.2.refs_0_
  350.7 4.7 skip_grad.3
  357.0 3.5 skip_back.2
  360.6 3.5 skip_back.3
  364.1 11.1 %collective-permute-done.51.came_ref = bf16[256,1152]{1,0:T(8,128)(2,1)S(1)} collective-permute-done((bf16[256,1152]{1,0:T(8,128)(2,1)S(1)}, bf16[256,1152]{1,0:T(8,128)(2,1)S(1)}, u32[]{:S(2)}, u32[]{:S(2)}) %collective-permute-start.51) | collective-permute-done | bytes 589856 | tf_op jit(solution)/shard_map/ppermute | solution.py:348
  378.4 7.8 %collective-permute-done.52.came_ref = bf16[128,1152]{1,0:T(8,128)(2,1)S(1)} collective-permute-done((bf16[128,1152]{1,0:T(8,128)(2,1)S(1)}, bf16[128,1152]{1,0:T(8,128)(2,1)S(1)}, u32[]{:S(2)}, u32[]{:S(2)}) %collective-permute-start.52) | collective-permute-done | bytes 294944 | tf_op jit(solution)/shard_map/ppermute | solution.py:348
  390.8 8.8 %collective-permute-done.53.came_ref = bf16[64,1152]{1,0:T(8,128)(2,1)S(1)} collective-permute-done((bf16[64,1152]{1,0:T(8,128)(2,1)S(1)}, bf16[64,1152]{1,0:T(8,128)(2,1)S(1)}, u32[]{:S(2)}, u32[]{:S(2)}) %collective-permute-start.53) | collective-permute-done | bytes 147488 | tf_op jit(solution)/shard_map/ppermute | solution.py:348
  399.7 3.5 collective-permute-start.54
  407.3 6.3 %collective-permute-done.54.came_ref = bf16[64,1152]{1,0:T(8,128)(2,1)S(1)} collective-permute-done((bf16[64,1152]{1,0:T(8,128)(2,1)S(1)}, bf16[64,1152]{1,0:T(8,128)(2,1)S(1)}, u32[]{:S(2)}, u32[]{:S(2)}) %collective-permute-start.54) | collective-permute-done | bytes 147488 | tf_op jit(solution)/shard_map/ppermute | solution.py:348
  423.6 10.3 %collective-permute-done.61.came_ref = bf16[128,1024]{1,0:T(8,128)(2,1)S(1)} collective-permute-done((bf16[128,1024]{1,0:T(8,128)(2,1)S(1)}, bf16[128,1024]{1,0:T(8,128)(2,1)S(1)}, u32[]{:S(2)}, u32[]{:S(2)}) %collective-permute-start.61) | collective-permute-done | bytes 262176 | tf_op jit(solution)/shard_map/ppermute | solution.py:348
  438.7 6.4 %collective-permute-done.62.came_ref = bf16[256,1024]{1,0:T(8,128)(2,1)S(1)} collective-permute-done((bf16[256,1024]{1,0:T(8,128)(2,1)S(1)}, bf16[256,1024]{1,0:T(8,128)(2,1)S(1)}, u32[]{:S(2)}, u32[]{:S(2)}) %collective-permute-start.62) | collective-permute-done | bytes 524320 | tf_op jit(solution)/shard_map/ppermute | solution.py:348
  446.3 4.6 collective-permute-done.58.came_ref
  457.8 12.9 %collective-permute-done.63.came_ref = bf16[512,1024]{1,0:T(8,128)(2,1)} collective-permute-done((bf16[512,1024]{1,0:T(8,128)(2,1)}, bf16[512,1024]{1,0:T(8,128)(2,1)}, u32[]{:S(2)}, u32[]{:S(2)}) %collective-permute-start.63) | collective-permute-done | bytes 1048608 | tf_op jit(solution)/shard_map/ppermute | solution.py:348
  (405 shorter events, 177.7 us)
Async XLA Ops:
  7.2 286.5 %reduce-scatter.2.cloned.1.call-start = ((), (), s32[]{:S(2)}) async-start(), calls=%async_computation.1 | async-start | bytes 4718592 | tf_op jit(solution)/shard_map/reduce_scatter | solution.py:962
  9.5 14.9 %collective-permute-start = (bf16[1024,256]{1,0:T(8,128)(2,1)S(1)}, bf16[1024,256]{1,0:T(8,128)(2,1)S(1)}, u32[]{:S(2)}, u32[]{:S(2)}) collective-permute-start(bf16[1024,256]{1,0:T(8,128)(2,1)S(1)} %bitcast.183), channel_id=1, source_target_pairs={{0,16},{16,0},{1,17},{17,1},{2,18},{18,2},{3,19},{19,3},{4,20},{20... | collective-permute-start | bytes 1572872 | tf_op jit(solution)/shard_map/ppermute | solution.py:348
  28.7 14.0 %collective-permute-start.6 = (bf16[1024,256]{1,0:T(8,128)(2,1)S(1)}, bf16[1024,256]{1,0:T(8,128)(2,1)}, u32[]{:S(2)}, u32[]{:S(2)}) collective-permute-start(bf16[1024,256]{1,0:T(8,128)(2,1)S(1)} %bitcast.182), channel_id=1, source_target_pairs={{0,16},{16,0},{1,17},{17,1},{2,18},{18,2},{3,19},{19,3},{4,20},{20... | collective-permute-start | bytes 1572872 | tf_op jit(solution)/shard_map/ppermute | solution.py:348
  30.9 25.3 %collective-permute-start.5 = (bf16[512,1024]{1,0:T(8,128)(2,1)S(1)}, bf16[512,1024]{1,0:T(8,128)(2,1)}, u32[]{:S(2)}, u32[]{:S(2)}) collective-permute-start(bf16[512,1024]{1,0:T(8,128)(2,1)S(1)} %add_convert_fusion.9.refs_1_.mine_ref), channel_id=1, source_target_pairs={{0,2},{1,3},{2,0},{3,1},{4,6},{5,7},{6,4},{7,5},{8,10},{9,11},{10,... | collective-permute-start | bytes 3145736 | tf_op jit(solution)/shard_map/ppermute | solution.py:348
  61.4 8.9 %collective-permute-start.11 = (bf16[512,1024]{1,0:T(8,128)(2,1)}, bf16[512,1024]{1,0:T(8,128)(2,1)}, u32[]{:S(2)}, u32[]{:S(2)}) collective-permute-start(bf16[512,1024]{1,0:T(8,128)(2,1)} %get-tuple-element.115.refs_0_), channel_id=1, source_target_pairs={{0,1},{1,0},{2,3},{3,2},{4,5},{5,4},{6,7},{7,6},{8,9},{9,8},{10,11... | collective-permute-start | bytes 3145736 | tf_op jit(solution)/shard_map/ppermute | solution.py:348
  61.4 25.6 %collective-permute-start.12 = (bf16[512,1024]{1,0:T(8,128)(2,1)S(1)}, bf16[512,1024]{1,0:T(8,128)(2,1)S(1)}, u32[]{:S(2)}, u32[]{:S(2)}) collective-permute-start(bf16[512,1024]{1,0:T(8,128)(2,1)S(1)} %add_convert_fusion.8.refs_2_.mine_ref), channel_id=1, source_target_pairs={{0,2},{1,3},{2,0},{3,1},{4,6},{5,7},{6,4},{7,5},{8,10},{9,11},{10,... | collective-permute-start | bytes 3145736 | tf_op jit(solution)/shard_map/ppermute | solution.py:348
  109.4 25.5 %collective-permute-start.18 = (bf16[512,1024]{1,0:T(8,128)(2,1)S(1)}, bf16[512,1024]{1,0:T(8,128)(2,1)S(1)}, u32[]{:S(2)}, u32[]{:S(2)}) collective-permute-start(bf16[512,1024]{1,0:T(8,128)(2,1)S(1)} %add_convert_fusion.7.refs_0_.mine_ref), channel_id=1, source_target_pairs={{0,2},{1,3},{2,0},{3,1},{4,6},{5,7},{6,4},{7,5},{8,10},{9,11},{10,... | collective-permute-start | bytes 3145736 | tf_op jit(solution)/shard_map/ppermute | solution.py:348
  136.2 25.6 %collective-permute-start.24 = (bf16[512,1024]{1,0:T(8,128)(2,1)S(1)}, bf16[512,1024]{1,0:T(8,128)(2,1)S(1)}, u32[]{:S(2)}, u32[]{:S(2)}) collective-permute-start(bf16[512,1024]{1,0:T(8,128)(2,1)S(1)} %add_convert_fusion.6.refs_1_.mine_ref), channel_id=1, source_target_pairs={{0,2},{1,3},{2,0},{3,1},{4,6},{5,7},{6,4},{7,5},{8,10},{9,11},{10,... | collective-permute-start | bytes 3145736 | tf_op jit(solution)/shard_map/ppermute | solution.py:348
  170.7 25.6 %collective-permute-start.34 = (bf16[512,1024]{1,0:T(8,128)(2,1)S(1)}, bf16[512,1024]{1,0:T(8,128)(2,1)S(1)}, u32[]{:S(2)}, u32[]{:S(2)}) collective-permute-start(bf16[512,1024]{1,0:T(8,128)(2,1)S(1)} %add_convert_fusion.5.refs_0_.mine_ref), channel_id=1, source_target_pairs={{0,2},{1,3},{2,0},{3,1},{4,6},{5,7},{6,4},{7,5},{8,10},{9,11},{10,... | collective-permute-start | bytes 3145736 | tf_op jit(solution)/shard_map/ppermute | solution.py:348
  201.4 253.2 %all-gather.2.cloned.1.call-start = ((), (), s32[]{:S(2)}) async-start(), calls=%async_computation.2 | async-start | bytes 4718592 | tf_op jit(solution)/shard_map/all_gather | solution.py:1023
  210.5 25.6 %collective-permute-start.35 = (bf16[512,1024]{1,0:T(8,128)(2,1)S(1)}, bf16[512,1024]{1,0:T(8,128)(2,1)S(1)}, u32[]{:S(2)}, u32[]{:S(2)}) collective-permute-start(bf16[512,1024]{1,0:T(8,128)(2,1)S(1)} %copy-done.5), channel_id=1, source_target_pairs={{0,2},{1,3},{2,0},{3,1},{4,6},{5,7},{6,4},{7,5},{8,10},{9,11},{10,... | collective-permute-start | bytes 3145736 | tf_op jit(solution)/shard_map/ppermute | solution.py:348
  262.1 25.3 %collective-permute-start.43 = (bf16[512,1024]{1,0:T(8,128)(2,1)S(1)}, bf16[512,1024]{1,0:T(8,128)(2,1)S(1)}, u32[]{:S(2)}, u32[]{:S(2)}) collective-permute-start(bf16[512,1024]{1,0:T(8,128)(2,1)S(1)} %add_convert_fusion.3.refs_11_.mine_ref), channel_id=1, source_target_pairs={{0,2},{1,3},{2,0},{3,1},{4,6},{5,7},{6,4},{7,5},{8,10},{9,11},{10,... | collective-permute-start | bytes 3145736 | tf_op jit(solution)/shard_map/ppermute | solution.py:348
  301.2 7.3 %collective-permute-start.40 = (bf16[512,1024]{1,0:T(8,128)(2,1)}, bf16[512,1024]{1,0:T(8,128)(2,1)}, u32[]{:S(2)}, u32[]{:S(2)}) collective-permute-start(bf16[512,1024]{1,0:T(8,128)(2,1)} %convolution_convert_fusion.3), channel_id=1, source_target_pairs={{0,1},{1,0},{2,3},{3,2},{4,5},{5,4},{6,7},{7,6},{8,9},{9,8},{10,11... | collective-permute-start | bytes 3145736 | tf_op jit(solution)/shard_map/ppermute | solution.py:348
  301.7 33.5 %collective-permute-start.42 = (bf16[512,1024]{1,0:T(8,128)(2,1)}, bf16[512,1024]{1,0:T(8,128)(2,1)S(1)}, u32[]{:S(2)}, u32[]{:S(2)}) collective-permute-start(bf16[512,1024]{1,0:T(8,128)(2,1)} %copy-done.49), channel_id=1, source_target_pairs={{0,2},{1,3},{2,0},{3,1},{4,6},{5,7},{6,4},{7,5},{8,10},{9,11},{10,... | collective-permute-start | bytes 3145736 | tf_op jit(solution)/shard_map/ppermute | solution.py:348
  303.2 30.6 %collective-permute-start.44 = (bf16[512,1024]{1,0:T(8,128)(2,1)}, bf16[512,1024]{1,0:T(8,128)(2,1)S(1)}, u32[]{:S(2)}, u32[]{:S(2)}) collective-permute-start(bf16[512,1024]{1,0:T(8,128)(2,1)} %copy-done.89), channel_id=1, source_target_pairs={{0,16},{16,0},{1,17},{17,1},{2,18},{18,2},{3,19},{19,3},{4,20},{20... | collective-permute-start | bytes 3145736 | tf_op jit(solution)/shard_map/ppermute | solution.py:348
  304.7 41.0 %collective-permute-start.48 = (bf16[512,1024]{1,0:T(8,128)(2,1)S(1)}, bf16[512,1024]{1,0:T(8,128)(2,1)}, u32[]{:S(2)}, u32[]{:S(2)}) collective-permute-start(bf16[512,1024]{1,0:T(8,128)(2,1)S(1)} %copy-done.8), channel_id=1, source_target_pairs={{0,1},{1,0},{2,3},{3,2},{4,5},{5,4},{6,7},{7,6},{8,9},{9,8},{10,11... | collective-permute-start | bytes 3145736 | tf_op jit(solution)/shard_map/ppermute | solution.py:348
  338.9 11.8 %collective-permute-start.47 = (bf16[512,1024]{1,0:T(8,128)(2,1)S(1)}, bf16[512,1024]{1,0:T(8,128)(2,1)}, u32[]{:S(2)}, u32[]{:S(2)}) collective-permute-start(bf16[512,1024]{1,0:T(8,128)(2,1)S(1)} %get-tuple-element.172.refs_2_.own_ref), channel_id=1, source_target_pairs={{0,1},{1,0},{2,3},{3,2},{4,5},{5,4},{6,7},{7,6},{8,9},{9,8},{10,11... | collective-permute-start | bytes 3145736 | tf_op jit(solution)/shard_map/ppermute | solution.py:348
  355.5 19.8 %collective-permute-start.51 = (bf16[256,1152]{1,0:T(8,128)(2,1)S(1)}, bf16[256,1152]{1,0:T(8,128)(2,1)S(1)}, u32[]{:S(2)}, u32[]{:S(2)}) collective-permute-start(bf16[256,1152]{1,0:T(8,128)(2,1)S(1)} %get-tuple-element.179), channel_id=1, source_target_pairs={{0,16},{16,0},{1,17},{17,1},{2,18},{18,2},{3,19},{19,3},{4,20},{20... | collective-permute-start | bytes 1769480 | tf_op jit(solution)/shard_map/ppermute | solution.py:348
  375.5 10.8 %collective-permute-start.52 = (bf16[128,1152]{1,0:T(8,128)(2,1)S(1)}, bf16[128,1152]{1,0:T(8,128)(2,1)S(1)}, u32[]{:S(2)}, u32[]{:S(2)}) collective-permute-start(bf16[128,1152]{1,0:T(8,128)(2,1)S(1)} %get-tuple-element.184), channel_id=1, source_target_pairs={{0,4},{4,0},{8,12},{12,8},{1,5},{5,1},{9,13},{13,9},{2,6},{6,2},{1... | collective-permute-start | bytes 884744 | tf_op jit(solution)/shard_map/ppermute | solution.py:348
  378.4 24.8 %collective-permute-start.59 = (bf16[256,1024]{1,0:T(8,128)(2,1)S(1)}, bf16[256,1024]{1,0:T(8,128)(2,1)S(1)}, u32[]{:S(2)}, u32[]{:S(2)}) collective-permute-start(bf16[256,1024]{1,0:T(8,128)(2,1)S(1)} %copy-done.91), channel_id=1, source_target_pairs={{0,4},{4,0},{8,12},{12,8},{1,5},{5,1},{9,13},{13,9},{2,6},{6,2},{1... | collective-permute-start | bytes 1572872 | tf_op jit(solution)/shard_map/ppermute | solution.py:348
  386.6 13.0 %collective-permute-start.53 = (bf16[64,1152]{1,0:T(8,128)(2,1)S(1)}, bf16[64,1152]{1,0:T(8,128)(2,1)S(1)}, u32[]{:S(2)}, u32[]{:S(2)}) collective-permute-start(bf16[64,1152]{1,0:T(8,128)(2,1)S(1)} %get-tuple-element.186), channel_id=1, source_target_pairs={{0,8},{4,12},{8,0},{12,4},{1,9},{5,13},{9,1},{13,5},{2,10},{6,14},... | collective-permute-start | bytes 442376 | tf_op jit(solution)/shard_map/ppermute | solution.py:348
  389.7 29.4 %collective-permute-start.57 = (bf16[1024,256]{1,0:T(8,128)(2,1)}, bf16[1024,256]{1,0:T(8,128)(2,1)S(1)}, u32[]{:S(2)}, u32[]{:S(2)}) collective-permute-start(bf16[1024,256]{1,0:T(8,128)(2,1)} %copy-done.75), channel_id=1, source_target_pairs={{0,16},{16,0},{1,17},{17,1},{2,18},{18,2},{3,19},{19,3},{4,20},{20... | collective-permute-start | bytes 1572872 | tf_op jit(solution)/shard_map/ppermute | solution.py:348
  399.7 13.9 %collective-permute-start.54 = (bf16[64,1152]{1,0:T(8,128)(2,1)S(1)}, bf16[64,1152]{1,0:T(8,128)(2,1)S(1)}, u32[]{:S(2)}, u32[]{:S(2)}) collective-permute-start(bf16[64,1152]{1,0:T(8,128)(2,1)S(1)} %fold.9.value_ref.refs_0_), channel_id=1, source_target_pairs={{0,8},{4,12},{8,0},{12,4},{1,9},{5,13},{9,1},{13,5},{2,10},{6,14},... | collective-permute-start | bytes 442376 | tf_op jit(solution)/shard_map/ppermute | solution.py:348
  404.8 14.2 %collective-permute-start.60 = (bf16[128,1024]{1,0:T(8,128)(2,1)}, bf16[128,1024]{1,0:T(8,128)(2,1)S(1)}, u32[]{:S(2)}, u32[]{:S(2)}) collective-permute-start(bf16[128,1024]{1,0:T(8,128)(2,1)} %get-tuple-element.192), channel_id=1, source_target_pairs={{0,8},{4,12},{8,0},{12,4},{1,9},{5,13},{9,1},{13,5},{2,10},{6,14},... | collective-permute-start | bytes 786440 | tf_op jit(solution)/shard_map/ppermute | solution.py:348
  404.9 17.1 %collective-permute-start.56 = (bf16[1024,256]{1,0:T(8,128)(2,1)S(1)}, bf16[1024,256]{1,0:T(8,128)(2,1)S(1)}, u32[]{:S(2)}, u32[]{:S(2)}) collective-permute-start(bf16[1024,256]{1,0:T(8,128)(2,1)S(1)} %get-tuple-element.180.refs_0_), channel_id=1, source_target_pairs={{0,16},{16,0},{1,17},{17,1},{2,18},{18,2},{3,19},{19,3},{4,20},{20... | collective-permute-start | bytes 1572872 | tf_op jit(solution)/shard_map/ppermute | solution.py:348
  404.9 30.1 %collective-permute-start.45 = (bf16[256,1024]{1,0:T(8,128)(2,1)}, bf16[256,1024]{1,0:T(8,128)(2,1)}, u32[]{:S(2)}, u32[]{:S(2)}) collective-permute-start(bf16[256,1024]{1,0:T(8,128)(2,1)} %get-tuple-element.173), channel_id=1, source_target_pairs={{0,2},{1,3},{2,0},{3,1},{4,6},{5,7},{6,4},{7,5},{8,10},{9,11},{10,... | collective-permute-start | bytes 1572872 | tf_op jit(solution)/shard_map/ppermute | solution.py:348
  414.3 20.7 %collective-permute-start.46 = (bf16[256,1024]{1,0:T(8,128)(2,1)}, bf16[256,1024]{1,0:T(8,128)(2,1)}, u32[]{:S(2)}, u32[]{:S(2)}) collective-permute-start(bf16[256,1024]{1,0:T(8,128)(2,1)} %get-tuple-element.174), channel_id=1, source_target_pairs={{0,2},{1,3},{2,0},{3,1},{4,6},{5,7},{6,4},{7,5},{8,10},{9,11},{10,... | collective-permute-start | bytes 1572872 | tf_op jit(solution)/shard_map/ppermute | solution.py:348
  419.0 15.0 %collective-permute-start.55 = (bf16[128,1152]{1,0:T(8,128)(2,1)S(1)}, bf16[128,1152]{1,0:T(8,128)(2,1)S(1)}, u32[]{:S(2)}, u32[]{:S(2)}) collective-permute-start(bf16[128,1152]{1,0:T(8,128)(2,1)S(1)} %join.6.value_ref.refs_0_), channel_id=1, source_target_pairs={{0,4},{4,0},{8,12},{12,8},{1,5},{5,1},{9,13},{13,9},{2,6},{6,2},{1... | collective-permute-start | bytes 884744 | tf_op jit(solution)/shard_map/ppermute | solution.py:348
  419.1 14.8 %collective-permute-start.61 = (bf16[128,1024]{1,0:T(8,128)(2,1)S(1)}, bf16[128,1024]{1,0:T(8,128)(2,1)S(1)}, u32[]{:S(2)}, u32[]{:S(2)}) collective-permute-start(bf16[128,1024]{1,0:T(8,128)(2,1)S(1)} %fold.11.value_ref), channel_id=1, source_target_pairs={{0,8},{4,12},{8,0},{12,4},{1,9},{5,13},{9,1},{13,5},{2,10},{6,14},... | collective-permute-start | bytes 786440 | tf_op jit(solution)/shard_map/ppermute | solution.py:348
  434.0 11.1 %collective-permute-start.62 = (bf16[256,1024]{1,0:T(8,128)(2,1)S(1)}, bf16[256,1024]{1,0:T(8,128)(2,1)S(1)}, u32[]{:S(2)}, u32[]{:S(2)}) collective-permute-start(bf16[256,1024]{1,0:T(8,128)(2,1)S(1)} %join.9.value_ref), channel_id=1, source_target_pairs={{0,4},{4,0},{8,12},{12,8},{1,5},{5,1},{9,13},{13,9},{2,6},{6,2},{1... | collective-permute-start | bytes 1572872 | tf_op jit(solution)/shard_map/ppermute | solution.py:348
  435.0 15.9 %collective-permute-start.58 = (bf16[256,1152]{1,0:T(8,128)(2,1)}, bf16[256,1152]{1,0:T(8,128)(2,1)}, u32[]{:S(2)}, u32[]{:S(2)}) collective-permute-start(bf16[256,1152]{1,0:T(8,128)(2,1)} %join.7.refs_2_.value_ref.refs_0_), channel_id=1, source_target_pairs={{0,16},{16,0},{1,17},{17,1},{2,18},{18,2},{3,19},{19,3},{4,20},{20... | collective-permute-start | bytes 1769480 | tf_op jit(solution)/shard_map/ppermute | solution.py:348
  446.2 24.5 %collective-permute-start.63 = (bf16[512,1024]{1,0:T(8,128)(2,1)}, bf16[512,1024]{1,0:T(8,128)(2,1)}, u32[]{:S(2)}, u32[]{:S(2)}) collective-permute-start(bf16[512,1024]{1,0:T(8,128)(2,1)} %join.10.value_ref), channel_id=1, source_target_pairs={{0,16},{16,0},{1,17},{17,1},{2,18},{18,2},{3,19},{19,3},{4,20},{20... | collective-permute-start | bytes 3145736 | tf_op jit(solution)/shard_map/ppermute | solution.py:348
  (140 other events, 887.1 us)
Sparse Core Ops, SparseCore 0:
  201.5 92.1 reduce-scatter.1
  296.1 84.9 all-gather.1
